TPU v7x, 256 devices: a whole 4x4x8 slice. The times are simulated.
256 devices in a mesh: row: 64 (over y, z, core), col: 4 (over x).
Axes of the slice: x: 4, y: 4, z: 8, core: 2. Of those that a mesh axis runs over, the one named last changes fastest.
Arguments:
- panel_matrix: float32 [65536, 512], P(('row', 'col')), may hold values from -1 to 1, as said below
- trailing: float32 [65536, 4096], P('row', 'col'), may hold values from -6 to 6
Outputs:
- r_factor: float32 [512, 512], replicated
- coupling: float32 [512, 4096], P(None, 'col')
- projected: float32 [65536, 4096], P('row', 'col')
Inputs may be any that keep to these rules, and one draw needn't show every extreme that they name: panel_matrix has full column rank 512.
All inputs are finite; a program needn't handle non-finite values.
Results may differ from a plain program's by a relative error of at most 0.000088.
Values sent between devices are 32-bit elements; how exact they have to be, the bound alone decides.
A program may use at most 64 MiB of HBM per device.

v0:
```python
import jax
import jax.numpy as jnp
from jax import lax
from jax.sharding import PartitionSpec as P

precise = lax.Precision.HIGHEST


def contract_rows(left, right):
    return lax.dot_general(
        left, right, (((0,), (0,)), ((), ())), precision=precise, preferred_element_type=jnp.float32
    )


def shards(panel_matrix, trailing):
    gram_part = contract_rows(panel_matrix, panel_matrix)
    gram = lax.psum(gram_part, ("row", "col"))
    lower_factor = jnp.linalg.cholesky(gram)
    local_basis = jax.scipy.linalg.solve_triangular(lower_factor, panel_matrix.T, lower=True).T
    basis_block = lax.all_gather(local_basis, "col", axis=0, tiled=True)
    coupling_part = contract_rows(basis_block, trailing)
    coupling = lax.psum(coupling_part, "row")
    update = jnp.dot(basis_block, coupling, precision=precise, preferred_element_type=jnp.float32)
    projected = trailing - update
    return (lower_factor.T, coupling, projected)


def solution(mesh):
    in_specs = (P(("row", "col"), None), P("row", "col"))
    out_specs = (P(), P(None, "col"), P("row", "col"))
    return jax.shard_map(shards, mesh=mesh, in_specs=in_specs, out_specs=out_specs, check_vma=False)
```

profile of v0, /device:TPU:1, one launch (start us, length us, event | category | flops | bytes accessed | tf_op | source)
XLA Modules:
  0.0 666.9 jit_solution(5836454247812896802)
XLA Ops:
  7.2 3.3 fusion.33
  10.6 261.7 %all-reduce.4.cloned.1.call-done = f32[512,512]{0,1:T(8,128)} async-done(((f32[512,512]{0,1:T(8,128)}), f32[512,512]{0,1:T(8,128)}) %all-reduce.4.cloned.1.call-update) | async-done | bytes 1048592 | tf_op jit(solution)/shard_map/psum | solution.py:17
  272.3 1.6 copy.6
  274.2 11.7 %cholesky.104 = f32[128,128]{1,0:T(8,128)S(1)} custom-call(f32[128,128]{1,0:T(8,128)S(1)} %cholesky.266), custom_call_target="Cholesky" | custom-call | tf_op jit(solution)/shard_map/jit(cholesky)/cholesky | solution.py:18
  285.9 9.8 %custom-call.31 = f32[1,128,128]{1,2,0:T(8,128)S(1)} custom-call(f32[1,128,128]{2,1,0:T(8,128)S(1)} %get-tuple-element.35), custom_call_target="InvertDiagBlocksLowerTriangular" | custom-call | tf_op jit(solution)/shard_map/jit(cholesky)/cholesky | solution.py:18
  296.6 11.7 %cholesky.217 = f32[128,128]{1,0:T(8,128)S(1)} custom-call(f32[128,128]{1,0:T(8,128)S(1)} %cholesky.270), custom_call_target="Cholesky" | custom-call | tf_op jit(solution)/shard_map/jit(cholesky)/cholesky | solution.py:18
  308.3 10.1 %custom-call.32 = f32[1,128,128]{1,2,0:T(8,128)S(1)} custom-call(f32[1,128,128]{2,1,0:T(8,128)S(1)} %get-tuple-element.32), custom_call_target="InvertDiagBlocksLowerTriangular" | custom-call | tf_op jit(solution)/shard_map/jit(cholesky)/cholesky | solution.py:18
  319.1 11.7 %cholesky.238 = f32[128,128]{1,0:T(8,128)S(1)} custom-call(f32[128,128]{1,0:T(8,128)S(1)} %cholesky.275), custom_call_target="Cholesky" | custom-call | tf_op jit(solution)/shard_map/jit(cholesky)/cholesky | solution.py:18
  330.8 0.6 compare_reduce_fusion.1
  331.5 9.8 %custom-call.33 = f32[1,128,128]{1,2,0:T(8,128)S(1)} custom-call(f32[1,128,128]{2,1,0:T(8,128)S(1)} %get-tuple-element.29), custom_call_target="InvertDiagBlocksLowerTriangular" | custom-call | tf_op jit(solution)/shard_map/jit(cholesky)/cholesky | solution.py:18
  341.9 11.7 %cholesky.255 = f32[128,128]{1,0:T(8,128)S(1)} custom-call(f32[128,128]{1,0:T(8,128)S(1)} %convolution_subtract_fusion.6), custom_call_target="Cholesky" | custom-call | tf_op jit(solution)/shard_map/jit(cholesky)/cholesky | solution.py:18
  353.7 0.7 compare_reduce_fusion
  354.4 0.6 compare_reduce_fusion.2
  357.7 1.4 fusion.1
  359.0 11.6 %while.1 = (s32[]{:T(128)}, f32[512,512]{1,0:T(8,128)}, s32[4,2]{0,1:T(2,128)S(1)}, f32[4,128,128]{2,1,0:T(8,128)S(1)}, s32[]{:T(128)}) while((s32[]{:T(128)}, f32[512,512]{1,0:T(8,128)}, s32[4,2]{0,1:T(2,128)S(1)}, f32[4,128,128]{2,1,0:T(8,128)S(1)}, s32[]{:T(128)}) %tuple.33), condition=%wide.while_cond, body=%wide.while_body.sunk | while | flops 2 | bytes 131189 | solution.py:19
  359.6 2.3 bitcast_dynamic-update-slice_fusion.2
  362.0 0.5 fusion.47
  362.6 2.3 bitcast_dynamic-update-slice_fusion.2
  365.5 2.3 bitcast_dynamic-update-slice_fusion.2
  367.9 0.5 fusion.47
  368.4 2.2 bitcast_dynamic-update-slice_fusion.2
  370.6 39.3 %custom-call.34 = f32[4,128,128]{1,2,0:T(8,128)S(1)} custom-call(f32[4,128,128]{2,1,0:T(8,128)S(1)} %get-tuple-element.10), custom_call_target="InvertDiagBlocksLowerTriangular" | custom-call | tf_op jit(solution)/shard_map/jit(_solve_triangular)/triangular_solve | solution.py:19
  410.3 1.2 convolution_subtract_fusion.5
  411.8 1.5 convolution_subtract_fusion.3
  413.6 1.7 convolution_subtract_fusion.2
  415.7 0.8 maximum_bitcast_fusion
  416.6 33.7 %all-gather.2.cloned.1.call-done = f32[1024,512]{0,1:T(8,128)} async-done(((f32[256,512]{0,1:T(8,128)}), f32[1024,512]{0,1:T(8,128)}) %all-gather.2.cloned.1.call-update) | async-done | bytes 2097168 | tf_op jit(solution)/shard_map/all_gather | solution.py:20
  450.3 10.2 %fusion.34 = f32[512,1024]{1,0:T(8,128)} fusion(f32[1024,512]{0,1:T(8,128)} %all-gather.2.cloned.1.call-done, f32[1024,1024]{1,0:T(8,128)} %param.3), kind=kOutput, calls=%fused_computation.71 | convolution fusion | flops 6442450944 | bytes 8388608 | tf_op jit(solution)/shard_map/dot_general | solution.py:10
  460.5 1.3 copy.7
  461.8 186.8 %all-reduce.6.cloned.1.call-done = f32[512,1024]{1,0:T(8,128)} async-done(((f32[512,1024]{1,0:T(8,128)}), f32[512,1024]{1,0:T(8,128)}) %all-reduce.6.cloned.1.call-update) | async-done | bytes 2097168 | tf_op jit(solution)/shard_map/psum | solution.py:22
  648.6 10.3 %convolution_subtract_fusion = f32[1024,1024]{1,0:T(8,128)} fusion(f32[1024,1024]{1,0:T(8,128)} %param.3, f32[1024,512]{0,1:T(8,128)S(1)} %copy-done.1, f32[512,1024]{1,0:T(8,128)} %all-reduce.6.cloned.1.call-done), kind=kOutput, calls=%fused_computation.2 | convolution fusion | flops 6443499520 | bytes 12582912 | tf_op jit(solution)/shard_map/dot_general | solution.py:23
  658.9 1.3 copy.26
  (42 shorter events, 5.1 us)
Async XLA Ops:
  7.2 265.1 %all-reduce.4.cloned.1.call-start = ((), (), s32[]{:S(2)}) async-start(), calls=%async_computation | async-start | bytes 2097152 | tf_op jit(solution)/shard_map/psum | solution.py:17
  10.5 439.8 %all-gather.2.cloned.1.call-start = ((), (), s32[]{:S(2)}) async-start(), calls=%async_computation.1 | async-start | bytes 2621440 | tf_op jit(solution)/shard_map/all_gather | solution.py:20
  272.3 1.7 copy-start.3
  341.9 68.0 %copy-start.2 = (f32[256,512]{1,0:T(8,128)S(1)}, f32[256,512]{1,0:T(8,128)}, u32[]{:S(2)}) copy-start(f32[256,512]{1,0:T(8,128)} %param.2) | copy-start | bytes 1572868
  416.6 232.0 %all-reduce.6.cloned.1.call-start = ((), (), s32[]{:S(2)}) async-start(), calls=%async_computation.2 | async-start | bytes 4194304 | tf_op jit(solution)/shard_map/psum | solution.py:22
  460.5 188.1 %copy-start.1 = (f32[1024,512]{0,1:T(8,128)S(1)}, f32[1024,512]{0,1:T(8,128)}, u32[]{:S(2)}) copy-start(f32[1024,512]{0,1:T(8,128)} %all-gather.2.cloned.1.call-done) | copy-start | bytes 6291460
  648.6 10.3 %copy-start = (f32[512,1024]{1,0:T(8,128)S(1)}, f32[512,1024]{1,0:T(8,128)}, u32[]{:S(2)}) copy-start(f32[512,1024]{1,0:T(8,128)} %all-reduce.6.cloned.1.call-done) | copy-start | bytes 6291460
Sparse Core Ops, SparseCore 0:
  14.0 258.2 all-reduce.3
  416.7 33.5 all-gather.1
  460.6 187.8 all-reduce.5
where the time goes:
time: 677 us; the launch traced here: 667 us
  waiting for transfers between devices  482 us (71%)
  other arithmetic  120 us (18%)
  matrix products  31.4 us (5%)
  between operations  16.8 us (2%)
  local copies, waits for them, and re-layouts  15.9 us (2%)
    psum x1, waiting for transfers between devices, shards(): gram = lax.psum(gram_part, ('row', 'col'))  262 us
    psum x1, waiting for transfers between devices, shards(): coupling = lax.psum(coupling_part, 'row')  187 us
    another operation x14, other arithmetic, shards(): lower_factor = jnp.linalg.cholesky(gram)  78.7 us
    another operation x3, other arithmetic, shards(): jax.scipy.linalg.solve_triangular(lower_factor, panel_matrix.T, lower=True)  40.7 us
    all_gather x1, waiting for transfers between devices, shards(): basis_block = lax.all_gather(local_basis, 'col', axis=0, tiled=True)  33.7 us
  transfers between devices with their start and end apart: 3, of which 3 were waited for; matrix products, arithmetic and copies ran while one was open for 0% of the time, Pallas kernels for 0%

commit v1 on v0

v1 whole, which is shorter than its diff:
```python
import jax
import jax.numpy as jnp
from jax import lax
from jax.experimental import pallas as pl
from jax.experimental.pallas import tpu as pltpu
from jax.sharding import PartitionSpec as P

HI = lax.Precision.HIGHEST
F32 = jnp.float32
BF16 = jnp.bfloat16
MESH = pl.DeviceIdType.MESH

NX, NY, NZ = 4, 4, 8
BLOCKS = [(i, j) for i in range(4) for j in range(i, 4)]
WP, WQ = 768, 256


def split(x):
    hi = x.astype(BF16)
    return hi, (x - hi.astype(F32)).astype(BF16)


def dot(a, b):
    return jnp.dot(a, b, preferred_element_type=F32)


def dot3(ah, al, bh, bl):
    return dot(ah, bh) + (dot(ah, bl) + dot(al, bh))


def dot_hi(a, b):
    return jnp.dot(a, b, precision=HI, preferred_element_type=F32)


def factor128(S, X):
    n = len(S)
    sub = lax.broadcasted_iota(jnp.int32, (8, 128), 0)
    S, X = list(S), list(X)
    for g in range(n):
        C = {}
        for h in range(g, n):
            for c in range(8):
                C[c, h] = jnp.broadcast_to(S[h][:, 8 * g + c : 8 * g + c + 1], (8, 128))
        D = jnp.zeros((8, 128), F32)
        for k in range(8):
            piv = jnp.broadcast_to(C[k, g][k : k + 1, :], (8, 128))
            rinv = 1.0 / piv
            D = jnp.where(sub == k, piv, D)
            row_s = jnp.broadcast_to(S[g][k : k + 1, :], (8, 128))
            row_x = jnp.broadcast_to(X[g][k : k + 1, :], (8, 128))
            row_c = {c: jnp.broadcast_to(C[c, g][k : k + 1, :], (8, 128)) for c in range(k + 1, 8)}
            for h in range(g, n):
                m = C[k, h]
                if h == g:
                    if k == 7:
                        continue
                    m = jnp.where(sub > k, m, 0.0)
                for c in range(k + 1, 8):
                    C[c, h] = C[c, h] - (m * row_c[c]) * rinv
                t = m * rinv
                S[h] = S[h] - t * row_s
                X[h] = X[h] - t * row_x
        scale = lax.rsqrt(D)
        S[g] = S[g] * scale
        X[g] = X[g] * scale
    return S, X


def chol_block(J, s_ref, r_ref, x_ref):
    o = pl.multiple_of(J * 128, 128)
    sub = lax.broadcasted_iota(jnp.int32, (8, 128), 0)
    lan = lax.broadcasted_iota(jnp.int32, (8, 128), 1)
    S = [s_ref[pl.ds(pl.multiple_of(o + 8 * g, 8), 8), pl.ds(o, 128)] for g in range(16)]
    X = [jnp.where(sub + 8 * g == lan, 1.0, 0.0).astype(F32) for g in range(16)]
    R, L = factor128(S, X)
    for g in range(16):
        rows = pl.ds(pl.multiple_of(o + 8 * g, 8), 8)
        r_ref[rows, pl.ds(o, 128)] = jnp.where(lan >= sub + 8 * g, R[g], 0.0)
        x_ref[rows, pl.ds(o, 128)] = L[g]


def chol_update(j, s_ref, r_ref, x_ref):
    a, b = j * 128, j * 128 + 128
    li = x_ref[a:b, a:b]
    if j > 0:
        x_ref[a:b, :a] = dot_hi(li, x_ref[a:b, :a])
    if j < 3:
        r12 = dot_hi(li, s_ref[a:b, b:])
        r_ref[a:b, b:] = r12
        r12t = r12.T
        for i in range(j + 1, 4):
            p, q = i * 128, i * 128 + 128
            left = r12t[p - b : q - b, :]
            s_ref[p:q, p:] = s_ref[p:q, p:] - dot_hi(left, r12[:, p - b :])
            x_ref[p:q, :b] = x_ref[p:q, :b] - dot_hi(left, x_ref[a:b, :b])


def comm_kernel(
    a_ref, t_ref,
    r_ref, x_ref, ag, wo_p, wo_q,
    s_ref, gb, gcl, ga, gl1p, gr1p, gl2p, gl1q, gr1q, gl2q, xb, go,
    wp_p, wp_q, wc_p, wc_q, wl1p, wr1p, wl2p, wl1q, wr1q, wl2q,
    send, recv, lsem,
):
    r = lax.axis_index("row")
    x = lax.axis_index("col")
    c = r % 2
    z = (r // 2) % NZ
    y = r // (2 * NZ)

    def at_y(d):
        return {"row": (((y + d) % NY) * NZ + z) * 2 + c}

    def at_z(d):
        return {"row": (y * NZ + (z + d) % NZ) * 2 + c}

    def at_x(d):
        return {"col": (x + d) % NX}

    sibling = {"row": r + 1 - 2 * c}
    axes = {"y": (NY, y, at_y), "z": (NZ, z, at_z)}

    counter = [0]

    def group(n):
        base = counter[0]
        counter[0] += n
        return base

    pending = []

    def copy(k, src, dst, to):
        return pltpu.make_async_remote_copy(
            src_ref=src, dst_ref=dst, send_sem=send.at[k], recv_sem=recv.at[k], device_id=to, device_id_type=MESH
        )

    def scatter(axis, buf, land, piece):
        n, i, at = axes[axis]
        base = group(n - 1)
        return [
            (lambda d=d: copy(base + d - 1, buf.at[pl.ds(((i + d) % n) * piece, piece)], land.at[d - 1], at(d)))
            for d in range(1, n)
        ]

    def gather(axis, buf, piece, start):
        n, i, at = axes[axis]
        base = group(n - 1)
        rows = pl.ds(start + i * piece, piece)
        return [(lambda d=d: copy(base + d - 1, buf.at[rows], buf.at[rows], at(d))) for d in range(1, n)]

    def single(src, dst, to):
        base = group(1)
        return [lambda: copy(base, src, dst, to)]

    def start(copies):
        for f in copies:
            f().start()
        pending.extend(copies)

    def arrive(copies):
        for f in copies:
            f().wait_recv()

    def reduce_into(axis, buf, land, piece):
        n, i, _ = axes[axis]
        total = buf[pl.ds(pl.multiple_of(i * piece, 8), piece), :]
        for d in range(n - 1):
            total = total + land[d]
        return total

    barrier = pltpu.get_barrier_semaphore()
    peers = [sibling] + [at_y(d) for d in range(1, NY)] + [at_z(d) for d in range(1, NZ)] + [at_x(d) for d in range(1, NX)]
    for p in peers:
        pl.semaphore_signal(barrier, inc=1, device_id=p, device_id_type=MESH)
    pl.semaphore_wait(barrier, len(peers))

    left, right = (x + NX - 1) % NX, (x + 1) % NX
    a_right = single(a_ref, ag.at[x], at_x(1))
    a_left = single(a_ref, ag.at[x], at_x(NX - 1))
    start(a_right)
    start(a_left)
    ag[x] = a_ref[...]

    a_own = a_ref[...]
    a_own_t = a_own.T
    for i in range(4):
        rows = dot_hi(a_own_t[i * 128 : i * 128 + 128], a_own[:, i * 128 :])
        for j in range(i, 4):
            n = BLOCKS.index((i, j))
            gb[n // 5, (n % 5) * 128 : (n % 5) * 128 + 128, :] = rows[:, (j - i) * 128 : (j - i) * 128 + 128]
    g_core = single(gb.at[1 - c], gcl, sibling)
    start(g_core)

    def w_block(b, first):
        ah, al = split(ag[b].T)

        def chunk(out, rows, cols):
            th, tl = split(t_ref[rows, cols])
            return dot3(ah, al, th, tl)

        rows = pl.ds(pl.multiple_of(b * 256, 256), 256)

        def add(ref, cols_out, v):
            for half in range(2):
                part = v[half * 256 : half * 256 + 256]
                if first:
                    ref[half, :, cols_out] = part
                else:
                    ref[half, :, cols_out] = ref[half, :, cols_out] + part

        def body(n, carry):
            cols = pl.ds(pl.multiple_of(n * 256, 256), 256)
            add(wp_p, cols, chunk(wp_p, rows, cols))
            return carry

        lax.fori_loop(0, WP // 256, body, 0)
        add(wp_q, pl.ds(0, WQ), chunk(wp_q, rows, pl.ds(WP, WQ)))

    w_block(x, True)

    arrive(g_core)
    ga[0:640] = gb[c, 0:640] + gcl[...]
    ga[640:768] = jnp.zeros((128, 128), F32)
    g1p = scatter("y", ga.at[0:512], gl1p, 128)
    g1q = scatter("z", ga.at[512:768], gl1q, 32)
    start(g1p)
    start(g1q)
    arrive(g1p)
    arrive(g1q)
    gr1p[...] = reduce_into("y", ga.at[0:512], gl1p, 128)
    gr1q[...] = reduce_into("z", ga.at[512:768], gl1q, 32)
    g2p = scatter("z", gr1p, gl2p, 16)
    g2q = scatter("y", gr1q, gl2q, 8)
    start(g2p)
    start(g2q)

    arrive(a_right)
    arrive(a_left)
    on_right = single(ag.at[left, 0:128], ag.at[left, 0:128], at_x(1))
    on_left = single(ag.at[right, 128:256], ag.at[right, 128:256], at_x(NX - 1))
    start(on_right)
    start(on_left)

    arrive(g2p)
    arrive(g2q)
    xb[x, 0:16] = reduce_into("z", gr1p, gl2p, 16)
    xb[x, 16:24] = reduce_into("y", gr1q, gl2q, 8)
    base = group(NX - 1)
    g_x = [(lambda d=d: copy(base + d - 1, xb.at[x], xb.at[x], at_x(d))) for d in range(1, NX)]
    start(g_x)
    w_block(left, False)
    arrive(g_x)
    total = (xb[0] + xb[1]) + (xb[2] + xb[3])
    go[c, pl.ds(pl.multiple_of(y * 128 + z * 16, 8), 16), :] = total[0:16]
    go[c, pl.ds(pl.multiple_of(512 + z * 32 + y * 8, 8), 8), :] = total[16:24]
    g3p = gather("z", go.at[c], 16, y * 128)
    g3q = gather("y", go.at[c], 8, 512 + z * 32)
    start(g3p)
    start(g3q)
    w_block(right, False)
    arrive(g3p)
    arrive(g3q)
    g4p = gather("y", go.at[c], 128, 0)
    g4q = gather("z", go.at[c], 32, 512)
    start(g4p)
    start(g4q)
    arrive(on_right)
    arrive(on_left)
    w_block((x + 2) % NX, False)
    w_core_p = single(wp_p.at[1 - c], wc_p, sibling)
    w_core_q = single(wp_q.at[1 - c], wc_q, sibling)
    start(w_core_p)
    start(w_core_q)
    arrive(g4p)
    arrive(g4q)
    g_core2 = single(go.at[c, 0:640], go.at[c, 0:640], sibling)
    start(g_core2)
    arrive(g_core2)
    for n, (i, j) in enumerate(BLOCKS):
        s_ref[i * 128 : i * 128 + 128, j * 128 : j * 128 + 128] = go[n // 5, (n % 5) * 128 : (n % 5) * 128 + 128, :]

    x_ref[...] = jnp.zeros_like(x_ref)
    r_ref[...] = jnp.zeros_like(r_ref)

    w1p = scatter("y", wp_p.at[c], wl1p, 64)
    w1q = scatter("z", wp_q.at[c], wl1q, 32)
    w2p = scatter("z", wr1p, wl2p, 8)
    w2q = scatter("y", wr1q, wl2q, 8)
    w3p = gather("z", wo_p.at[c], 8, y * 64)
    w3q = gather("y", wo_q.at[c], 8, z * 32)
    w4p = gather("y", wo_p.at[c], 64, 0)
    w4q = gather("z", wo_q.at[c], 32, 0)
    w5p = single(wo_p.at[c], wo_p.at[c], sibling)
    w5q = single(wo_q.at[c], wo_q.at[c], sibling)

    def w_step(j):
        if j == 0:
            arrive(w_core_p)
            arrive(w_core_q)
            wp_p[c] = wp_p[c] + wc_p[...]
            wp_q[c] = wp_q[c] + wc_q[...]
            start(w1p)
            start(w1q)
        if j == 1:
            arrive(w1p)
            arrive(w1q)
            wr1p[...] = reduce_into("y", wp_p.at[c], wl1p, 64)
            wr1q[...] = reduce_into("z", wp_q.at[c], wl1q, 32)
            start(w2p)
            start(w2q)
        if j == 2:
            arrive(w2p)
            arrive(w2q)
            wo_p[c, pl.ds(pl.multiple_of(y * 64 + z * 8, 8), 8), :] = reduce_into("z", wr1p, wl2p, 8)
            wo_q[c, pl.ds(pl.multiple_of(z * 32 + y * 8, 8), 8), :] = reduce_into("y", wr1q, wl2q, 8)
            start(w3p)
            start(w3q)
        if j == 3:
            arrive(w3p)
            arrive(w3q)
            start(w4p)
            start(w4q)

    def step(J, carry):
        for j in range(4):

            @pl.when(J == j)
            def _():
                w_step(j)

        chol_block(J, s_ref, r_ref, x_ref)
        for j in range(4):

            @pl.when(J == j)
            def _():
                chol_update(j, s_ref, r_ref, x_ref)

        return carry

    lax.fori_loop(0, 4, step, 0)

    arrive(w4p)
    arrive(w4q)
    start(w5p)
    start(w5q)
    arrive(w5p)
    arrive(w5q)
    for f in pending:
        f().wait_send()


def tail_kernel(t_ref, a_ref, x_ref, wp_ref, wq_ref, coupling_ref, out_ref, yh, yl):
    @pl.when(pl.program_id(0) == 0)
    def _():
        x = x_ref[...]
        xh, xl = split(x)
        xth, xtl = split(x.T)
        for n in range(4):
            if n < 3:
                w = jnp.concatenate([wp_ref[0, :, n * 256 : n * 256 + 256], wp_ref[1, :, n * 256 : n * 256 + 256]], 0)
            else:
                w = jnp.concatenate([wq_ref[0], wq_ref[1]], 0)
            wh, wl = split(w)
            cpl = dot3(xh, xl, wh, wl)
            coupling_ref[:, n * 256 : n * 256 + 256] = cpl
            ch, cl = split(cpl)
            yy = dot3(xth, xtl, ch, cl)
            h, l = split(yy)
            yh[:, n * 256 : n * 256 + 256] = h
            yl[:, n * 256 : n * 256 + 256] = l

    ah, al = split(a_ref[...])
    for n in range(4):
        cols = slice(n * 256, n * 256 + 256)
        out_ref[:, cols] = t_ref[:, cols] - dot3(ah, al, yh[:, cols], yl[:, cols])


def shards(panel_matrix, trailing):
    V = pl.BlockSpec(memory_space=pltpu.VMEM)
    f = lambda *s: jax.ShapeDtypeStruct(s, F32)
    v = lambda *s: pltpu.VMEM(s, F32)
    r, linv, ag, wo_p, wo_q = pl.pallas_call(
        comm_kernel,
        out_shape=(f(512, 512), f(512, 512), f(4, 256, 512), f(2, 256, WP), f(2, 256, WQ)),
        in_specs=[V, V],
        out_specs=(V,) * 5,
        scratch_shapes=[
            v(512, 512), v(2, 640, 128), v(640, 128), v(768, 128),
            v(3, 128, 128), v(128, 128), v(7, 16, 128),
            v(7, 32, 128), v(32, 128), v(3, 8, 128),
            v(4, 24, 128), v(2, 768, 128),
            v(2, 256, WP), v(2, 256, WQ), v(256, WP), v(256, WQ),
            v(3, 64, WP), v(64, WP), v(7, 8, WP),
            v(7, 32, WQ), v(32, WQ), v(3, 8, WQ),
            pltpu.SemaphoreType.DMA((110,)), pltpu.SemaphoreType.DMA((110,)), pltpu.SemaphoreType.DMA((2,)),
        ],
        name="reduce_and_factor",
        compiler_params=pltpu.CompilerParams(collective_id=0, has_side_effects=True, vmem_limit_bytes=48 * 2**20),
    )(panel_matrix, trailing)

    whole = lambda *s: pl.BlockSpec(s, lambda i: (0,) * len(s))
    coupling, projected = pl.pallas_call(
        tail_kernel,
        grid=(4,),
        out_shape=(f(512, 1024), f(1024, 1024)),
        in_specs=[
            pl.BlockSpec((256, 1024), lambda i: (i, 0)),
            pl.BlockSpec((None, 256, 512), lambda i: (i, 0, 0)),
            whole(512, 512),
            whole(2, 256, WP),
            whole(2, 256, WQ),
        ],
        out_specs=(whole(512, 1024), pl.BlockSpec((256, 1024), lambda i: (i, 0))),
        scratch_shapes=[pltpu.VMEM((512, 1024), BF16), pltpu.VMEM((512, 1024), BF16)],
        name="project",
        compiler_params=pltpu.CompilerParams(vmem_limit_bytes=48 * 2**20),
    )(trailing, ag, linv, wo_p, wo_q)
    return r, coupling, projected


def solution(mesh):
    in_specs = (P(("row", "col"), None), P("row", "col"))
    out_specs = (P(), P(None, "col"), P("row", "col"))
    return jax.shard_map(shards, mesh=mesh, in_specs=in_specs, out_specs=out_specs, check_vma=False)
```

time: 677 us -> 102 us (0.15); the launches traced: 667 us -> 102 us
  waiting for transfers between devices: 482 us -> 0 us
  other arithmetic: 120 us -> 0 us
  Pallas kernels: 0 us -> 97.6 us
  matrix products: 31.4 us -> 0 us
  between operations: 16.8 us -> 0.66 us
  local copies, waits for them, and re-layouts: 15.9 us -> 3.59 us
    psum x2 -> x0, waiting for transfers between devices: 448 us -> none  [the longest x1 262 us: shards(): gram = lax.psum(gram_part, ('row', 'col'))]
    another operation x17 -> x0, other arithmetic: 119 us -> none  [the longest x14 78.7 us: shards(): lower_factor = jnp.linalg.cholesky(gram)]
    pallas_call x0 -> x2, Pallas kernels: none -> 97.6 us  [the longest x1 86.5 us: shards(): pl.pallas_call(comm_kernel, out_shape=(f(512, 512), f(512, 512), f(4, 256...]
    all_gather x1 -> x0, waiting for transfers between devices: 33.7 us -> none  [shards(): basis_block = lax.all_gather(local_basis, 'col', axis=0, tiled=True)]
    dot_general x3 -> x0, matrix products: 23.8 us -> none  [the longest x2 13.5 us: contract_rows(): lax.dot_general(left, right, (((0,), (0,)), ((), ())), precision=precise,...]
    another operation x17 -> x0, local copies, waits for them, and re-layouts: 11.6 us -> none
    another operation x13 -> x0, matrix products: 7.58 us -> none  [the longest x7 5.71 us: shards(): jax.scipy.linalg.solve_triangular(lower_factor, panel_matrix.T, lower=True)]
  transfers between devices with their start and end apart: 3 -> 0, of which waited for: 3 -> 0; matrix products, arithmetic and copies ran while one was open for 0% -> 0% of each run, Pallas kernels for 0% -> 0%
where the time goes in v1:
time: 102 us
  Pallas kernels  97.6 us (96%)
  local copies, waits for them, and re-layouts  3.59 us (4%)
    pallas_call x1, Pallas kernels, shards(): pl.pallas_call(comm_kernel, out_shape=(f(512, 512), f(512, 512), f(4, 256...  86.5 us
    pallas_call x1, Pallas kernels, shards(): pl.pallas_call(tail_kernel, grid=(4,), out_shape=(f(512, 1024), f(1024, 1...  11.2 us
    unnamed x5, local copies, waits for them, and re-layouts  3.59 us

profile of v1, /device:TPU:1, one launch (start us, length us, event | category | flops | bytes accessed | tf_op | source)
XLA Modules:
  0.0 101.9 jit_solution(15606577400297005713)
XLA Ops:
  0.6 0.0 copy-start.1
  0.6 1.0 %copy-done.1 = f32[256,512]{1,0:T(8,128)S(1)} copy-done((f32[256,512]{1,0:T(8,128)S(1)}, f32[256,512]{1,0:T(8,128)}, u32[]{:S(2)}) %copy-start.1) | copy-done | bytes 524312
  1.7 86.5 %reduce_and_factor.1 = (f32[512,512]{1,0:T(8,128)S(1)}, f32[512,512]{1,0:T(8,128)S(1)}, f32[4,256,512]{2,1,0:T(8,128)}, f32[2,256,768]{2,1,0:T(8,128)S(1)}, f32[2,256,256]{2,1,0:T(8,128)S(1)}) custom-call(f32[256,512]{1,0:T(8,128)S(1)} %copy-done.1, f32[1024,1024]{1,0:T(8,128)} %t_ref.3), custom_call_target="tpu_custom_call" | custom-call | tf_op jit(solution)/shard_map/reduce_and_factor/pallas_call | solution.py:382
  88.1 0.0 copy-start
  88.1 1.6 %copy-done = f32[4,256,512]{2,1,0:T(8,128)S(1)} copy-done((f32[4,256,512]{2,1,0:T(8,128)S(1)}, f32[4,256,512]{2,1,0:T(8,128)}, u32[]{:S(2)}) %copy-start) | copy-done | bytes 2097176
  89.7 11.2 %project.1 = (f32[512,1024]{1,0:T(8,128)}, f32[1024,1024]{1,0:T(8,128)}) custom-call(f32[1024,1024]{1,0:T(8,128)} %t_ref.3, f32[4,256,512]{2,1,0:T(8,128)S(1)} %copy-done, f32[512,512]{1,0:T(8,128)S(1)} %get-tuple-element.12.x_ref, f32[2,256,768]{2,1,0:T(8,128)S(1)} %get-tuple-element.13.wp_ref, f32[2,256,256]{2,1,0:T(8,128)S(1)} %get-tuple-element.14.wq_ref), custom_call_target="tpu_custom_call" | custom-call | tf_op jit(solution)/shard_map/project/pallas_call | solution.py:402
  100.9 1.0 copy.6
Async XLA Ops:
  0.6 1.0 %copy-start.1 = (f32[256,512]{1,0:T(8,128)S(1)}, f32[256,512]{1,0:T(8,128)}, u32[]{:S(2)}) copy-start(f32[256,512]{1,0:T(8,128)} %a_ref.1) | copy-start | bytes 1572868
  88.1 1.6 %copy-start = (f32[4,256,512]{2,1,0:T(8,128)S(1)}, f32[4,256,512]{2,1,0:T(8,128)}, u32[]{:S(2)}) copy-start(f32[4,256,512]{2,1,0:T(8,128)} %get-tuple-element.11.a_ref) | copy-start | bytes 6291460

commit v2 on v0

v2 whole, which is shorter than its diff:
```python
import jax
import jax.numpy as jnp
from jax import lax
from jax.experimental import pallas as pl
from jax.experimental.pallas import tpu as pltpu
from jax.sharding import PartitionSpec as P

HI = lax.Precision.HIGHEST
F32 = jnp.float32
BF16 = jnp.bfloat16
MESH = pl.DeviceIdType.MESH
B8 = (8, 128)

NX, NY, NZ = 4, 4, 8
BLOCKS0 = [(0, 0), (0, 1), (0, 2), (0, 3)]
BLOCKS1 = [(1, 1), (1, 2), (1, 3), (2, 2), (2, 3), (3, 3)]
WP = 768


def split(x):
    hi = x.astype(BF16)
    return hi, (x - hi.astype(F32)).astype(BF16)


def dot(a, b):
    return jnp.dot(a, b, preferred_element_type=F32)


def dot3(ah, al, bh, bl):
    return dot(ah, bh) + (dot(ah, bl) + dot(al, bh))


def dot_hi(a, b):
    return jnp.dot(a, b, precision=HI, preferred_element_type=F32)


def bc(v):
    return jnp.broadcast_to(v, B8)


def factor128(block):
    n, nb = 16, 8
    sub = lax.broadcasted_iota(jnp.int32, B8, 0)
    lan = lax.broadcasted_iota(jnp.int32, B8, 1)
    S = [block[8 * g : 8 * g + 8] for g in range(n)]
    X = [jnp.where(sub + 8 * g == lan, 1.0, 0.0).astype(F32) for g in range(n)]
    for b in range(0, n, nb):
        e = b + nb
        own = None
        for g in range(b, e):
            if own is None:
                own = [bc(S[g][:, 8 * g + c : 8 * g + c + 1]) for c in range(8)]
            C = {(c, g): own[c] for c in range(8)}
            N = None
            if g + 1 < e:
                N = [bc(S[g + 1][:, 8 * (g + 1) + c : 8 * (g + 1) + c + 1]) for c in range(8)]
            for h in range(g + 1, e):
                for c in range(8):
                    C[c, h] = bc(S[h][:, 8 * g + c : 8 * g + c + 1])
            D = jnp.zeros(B8, F32)
            for k in range(8):
                piv = bc(C[k, g][k : k + 1, :])
                rinv = 1.0 / piv
                D = jnp.where(sub == k, piv, D)
                row_s, row_x = bc(S[g][k : k + 1, :]), bc(X[g][k : k + 1, :])
                row_c = {c: bc(C[c, g][k : k + 1, :]) for c in range(k + 1, 8)}
                for h in range(g, e):
                    m = C[k, h]
                    if h == g:
                        if k == 7:
                            continue
                        m = jnp.where(sub > k, m, 0.0)
                        for c in range(k + 1, 8):
                            C[c, h] = C[c, h] - (m * row_c[c]) * rinv
                        t = m * rinv
                    else:
                        t = m * rinv
                        for c in range(k + 1, 8):
                            C[c, h] = C[c, h] - t * row_c[c]
                        if h == g + 1:
                            for c in range(8):
                                N[c] = N[c] - t * bc(m[c : c + 1, :])
                    S[h] = S[h] - t * row_s
                    X[h] = X[h] - t * row_x
            own = N
            scale = lax.rsqrt(D)
            S[g] = S[g] * scale
            X[g] = X[g] * scale
        if e < n:
            U = jnp.concatenate(S[b:e], 0)
            both = jnp.concatenate([U, jnp.concatenate(X[b:e], 0)], 1)
            up = dot_hi(U.T[8 * e :], both)
            for h in range(e, n):
                S[h] = S[h] - up[8 * (h - e) : 8 * (h - e) + 8, :128]
                X[h] = X[h] - up[8 * (h - e) : 8 * (h - e) + 8, 128:]
    R = [jnp.where(lan >= sub + 8 * g, S[g], 0.0) for g in range(n)]
    return jnp.concatenate(R, 0), jnp.concatenate(X, 0)


def comm_kernel(
    a_hbm, t_hbm,
    r_ref, p_ref, qh_ref, ql_ref, cpl_ref,
    ag, t_ref, th, tl, s_ref, x_ref, gb0, gb1, gc0, gc1, ga0, ga1,
    gl10, gr10, gl20, gl11, gr11, gl21, xb0, xb1, go0, go1,
    w_ref, wc, wo, wl1p, wr1p, wl2p, wl1q, wr1q, wl2q,
    send, recv, lsem,
):
    r = lax.axis_index("row")
    x = lax.axis_index("col")
    c = r % 2
    z = (r // 2) % NZ
    y = r // (2 * NZ)

    def at_y(d):
        return {"row": (((y + d) % NY) * NZ + z) * 2 + c}

    def at_z(d):
        return {"row": (y * NZ + (z + d) % NZ) * 2 + c}

    def at_x(d):
        return {"col": (x + d) % NX}

    sibling = {"row": r + 1 - 2 * c}
    axes = {"x": (NX, x, at_x), "y": (NY, y, at_y), "z": (NZ, z, at_z)}
    counter = [0]
    pending = []

    def copies(pairs):
        base = counter[0]
        counter[0] += len(pairs)

        def make(k, src, dst, to):
            return lambda: pltpu.make_async_remote_copy(
                src_ref=src, dst_ref=dst, send_sem=send.at[k], recv_sem=recv.at[k], device_id=to, device_id_type=MESH
            )

        return [make(base + k, *p) for k, p in enumerate(pairs)]

    def start(group):
        for f in group:
            f().start()
        pending.extend(group)

    def arrive(group):
        for f in group:
            f().wait_recv()

    def rows_of(n):
        return lambda i: (pl.ds(pl.multiple_of(i * n, 8), n), slice(None))

    def halves_of(cols):
        return lambda i: (pl.ds(pl.multiple_of(i // 2 * 8, 8), 8), pl.ds(pl.multiple_of(i % 2 * cols, 128), cols))

    def scatter(axis, ref, piece, land):
        n, i, at = axes[axis]
        return copies([(ref.at[piece((i + d) % n)], land.at[d - 1], at(d)) for d in range(1, n)])

    def summed(axis, ref, piece, land):
        n, i, _ = axes[axis]
        total = ref[piece(i)]
        for d in range(n - 1):
            total = total + land[d]
        return total

    def gather(axis, ref, piece):
        n, i, at = axes[axis]
        return copies([(ref.at[piece(i)], ref.at[piece(i)], at(d)) for d in range(1, n)])

    barrier = pltpu.get_barrier_semaphore()
    peers = [sibling] + [at_y(d) for d in range(1, NY)] + [at_z(d) for d in range(1, NZ)] + [at_x(d) for d in range(1, NX)]
    for p in peers:
        pl.semaphore_signal(barrier, inc=1, device_id=p, device_id_type=MESH)
    load_a = pltpu.make_async_copy(a_hbm, ag.at[x], lsem.at[0])
    load_t = pltpu.make_async_copy(t_hbm, t_ref, lsem.at[1])
    load_a.start()
    load_t.start()
    load_a.wait()

    a_own = ag[x]
    a_own_t = a_own.T
    for i in range(4):
        rows = dot_hi(a_own_t[i * 128 : i * 128 + 128], a_own[:, i * 128 :])
        for j in range(i, 4):
            part = rows[:, (j - i) * 128 : (j - i) * 128 + 128]
            if i == 0:
                n = BLOCKS0.index((i, j))
                gb0[n // 2, n % 2 * 128 : n % 2 * 128 + 128, :] = part
            else:
                n = BLOCKS1.index((i, j))
                gb1[n // 3, n % 3 * 128 : n % 3 * 128 + 128, :] = part

    pl.semaphore_wait(barrier, len(peers))

    g0_c = copies([(gb0.at[1 - c], gc0, sibling)])
    g1_c = copies([(gb1.at[1 - c], gc1, sibling)])
    start(g0_c)
    start(g1_c)
    left, right, opposite = (x + NX - 1) % NX, (x + 1) % NX, (x + 2) % NX
    half = [slice(0, 256), slice(256, 512)]
    a1 = [
        copies([(ag.at[x, :, half[k]], ag.at[x, :, half[k]], at_x(1)), (ag.at[x, :, half[k]], ag.at[x, :, half[k]], at_x(NX - 1))])
        for k in range(2)
    ]
    a2 = [
        copies([
            (ag.at[left, 0:128, half[k]], ag.at[left, 0:128, half[k]], at_x(1)),
            (ag.at[right, 128:256, half[k]], ag.at[right, 128:256, half[k]], at_x(NX - 1)),
        ])
        for k in range(2)
    ]
    start(a1[0])
    start(a1[1])

    def w_block(b, k, first=False):
        ah, al = split(ag[b, :, half[k]].T)
        rows = pl.ds(pl.multiple_of(b * 256, 256), 256)
        for n in range(4):
            cols = slice(n * 256, n * 256 + 256)
            v = dot3(ah, al, th[rows, cols], tl[rows, cols])
            for m in range(2):
                part = v[m * 128 : m * 128 + 128]
                w_ref[k, m, :, cols] = part if first else w_ref[k, m, :, cols] + part

    s10 = scatter("y", ga0, rows_of(64), gl10)
    s20 = scatter("z", gr10, rows_of(8), gl20)
    s11 = scatter("z", ga1, rows_of(64), gl11)
    s21 = scatter("y", gr11, rows_of(16), gl21)
    x0 = copies([(xb0.at[x], xb0.at[x], at_x(d)) for d in range(1, NX)])
    x1 = copies([(xb1.at[x], xb1.at[x], at_x(d)) for d in range(1, NX)])
    o20 = gather("z", go0.at[c], lambda i: (pl.ds(pl.multiple_of(y * 64 + i * 8, 8), 8), slice(None)))
    o10 = gather("y", go0.at[c], rows_of(64))
    o21 = gather("y", go1.at[c], lambda i: (pl.ds(pl.multiple_of(z * 64 + i * 16, 8), 16), slice(None)))
    o11 = gather("z", go1.at[c], rows_of(64))
    o_c0 = copies([(go0.at[c], go0.at[c], sibling)])
    o_c1 = copies([(go1.at[c, 0:384], go1.at[c, 0:384], sibling)])

    zp, zq = halves_of(384), halves_of(128)
    wk = [w_ref.at[k, c] for k in range(2)]
    ok = [wo.at[k, c] for k in range(2)]
    wp, wq = [f.at[:, 0:WP] for f in wk], [f.at[:, WP:1024] for f in wk]
    op, oq = [f.at[:, 0:WP] for f in ok], [f.at[:, WP:1024] for f in ok]
    w_c = [copies([(w_ref.at[k, 1 - c], wc.at[k], sibling)]) for k in range(2)]
    w1 = [scatter("y", wp[k], rows_of(32), wl1p.at[k]) + scatter("z", wq[k], rows_of(16), wl1q.at[k]) for k in range(2)]
    w2 = [scatter("z", wr1p.at[k], zp, wl2p.at[k]) + scatter("y", wr1q.at[k], zq, wl2q.at[k]) for k in range(2)]

    def piece_p(i):
        return (pl.ds(pl.multiple_of(y * 32 + i // 2 * 8, 8), 8), pl.ds(pl.multiple_of(i % 2 * 384, 128), 384))

    def piece_q(i):
        return (pl.ds(pl.multiple_of(z * 16 + i // 2 * 8, 8), 8), pl.ds(pl.multiple_of(i % 2 * 128, 128), 128))

    w3 = [gather("z", op[k], piece_p) + gather("y", oq[k], piece_q) for k in range(2)]
    w4 = [gather("y", op[k], rows_of(32)) + gather("z", oq[k], rows_of(16)) for k in range(2)]
    w5 = [copies([(ok[k], ok[k], sibling)]) for k in range(2)]

    def w_core(k):
        arrive(w_c[k])
        w_ref[k, c] = w_ref[k, c] + wc[k]
        start(w1[k])

    def w_first(k):
        arrive(w1[k])
        wr1p[k] = summed("y", wp[k], rows_of(32), wl1p.at[k])
        wr1q[k] = summed("z", wq[k], rows_of(16), wl1q.at[k])
        start(w2[k])

    def w_second(k):
        arrive(w2[k])
        op[k][piece_p(z)] = summed("z", wr1p.at[k], zp, wl2p.at[k])
        oq[k][piece_q(y)] = summed("y", wr1q.at[k], zq, wl2q.at[k])
        start(w3[k])

    def w_third(k):
        arrive(w3[k])
        start(w4[k])

    def w_last(k):
        arrive(w4[k])
        start(w5[k])

    arrive(g0_c)
    ga0[...] = gb0[c] + gc0[...]
    start(s10)
    arrive(g1_c)
    ga1[0:384] = gb1[c] + gc1[...]
    ga1[384:512] = jnp.zeros((128, 128), F32)
    start(s11)

    load_t.wait()
    th[...], tl[...] = split(t_ref[...])
    w_block(x, 0, True)

    arrive(s10)
    gr10[...] = summed("y", ga0, rows_of(64), gl10)
    start(s20)
    arrive(s11)
    gr11[...] = summed("z", ga1, rows_of(64), gl11)
    start(s21)
    arrive(a1[0])
    start(a2[0])
    w_block(left, 0)
    arrive(s20)
    xb0[x] = summed("z", gr10, rows_of(8), gl20)
    start(x0)
    arrive(s21)
    xb1[x] = summed("y", gr11, rows_of(16), gl21)
    start(x1)
    w_block(right, 0)
    arrive(a1[1])
    start(a2[1])
    arrive(x0)
    go0[c, pl.ds(pl.multiple_of(y * 64 + z * 8, 8), 8), :] = (xb0[0] + xb0[1]) + (xb0[2] + xb0[3])
    start(o20)
    arrive(x1)
    go1[c, pl.ds(pl.multiple_of(z * 64 + y * 16, 8), 16), :] = (xb1[0] + xb1[1]) + (xb1[2] + xb1[3])
    start(o21)
    arrive(a2[0])
    w_block(opposite, 0)
    start(w_c[0])
    w_block(x, 1, True)
    arrive(o20)
    start(o10)
    arrive(o21)
    start(o11)
    w_core(0)
    w_block(left, 1)
    w_block(right, 1)
    arrive(o10)
    start(o_c0)
    arrive(a2[1])
    w_block(opposite, 1)
    start(w_c[1])
    arrive(o_c0)
    for n, (i, j) in enumerate(BLOCKS0):
        s_ref[:128, j * 128 : j * 128 + 128] = go0[n // 2, n % 2 * 128 : n % 2 * 128 + 128, :]
    r_ref[...] = jnp.zeros_like(r_ref)
    x_ref[...] = jnp.zeros_like(x_ref)
    arrive(o11)
    start(o_c1)
    w_core(1)

    diag = s_ref[0:128, 0:128]
    for J in range(4):
        a, b, q = J * 128, J * 128 + 128, J * 128 + 256
        r11, li = factor128(diag)
        r_ref[a:b, a:b] = r11
        x_ref[a:b, a:b] = li
        if J == 0:
            arrive(o_c1)
            for n, (i, j) in enumerate(BLOCKS1):
                s_ref[i * 128 : i * 128 + 128, j * 128 : j * 128 + 128] = go1[n // 3, n % 3 * 128 : n % 3 * 128 + 128, :]
            w_first(0)
        if J == 1:
            w_first(1)
            w_second(0)
        if J == 2:
            w_third(0)
            w_second(1)
        if J < 3:
            r12 = dot_hi(li, s_ref[a:b, b:q])
            r_ref[a:b, b:q] = r12
            diag = s_ref[b:q, b:q] - dot_hi(r12.T, r12)
            if J < 2:
                r13 = dot_hi(li, s_ref[a:b, q:])
                r_ref[a:b, q:] = r13
                s_ref[b:q, q:] = s_ref[b:q, q:] - dot_hi(r12.T, r13)
                s_ref[q:, q:] = s_ref[q:, q:] - dot_hi(r13.T, r13)
        if J > 0:
            x_ref[a:b, :a] = dot_hi(li, x_ref[a:b, :a])
        if J < 3:
            x_ref[b:, :b] = x_ref[b:, :b] - dot_hi(r_ref[a:b, b:].T, x_ref[a:b, :b])
    w_third(1)

    xi = x_ref[...]
    xh, xl = split(xi)
    xth, xtl = split(xi.T)

    def basis(rows, cols):
        ah, al = split(ag[rows][:, : cols.stop])
        return split(dot3(ah, al, xth[: cols.stop, cols], xtl[: cols.stop, cols]))

    qa = [basis(b, half[0]) for b in range(4)]
    for b in range(4):
        qh_ref[b], ql_ref[b] = basis(b, half[1])
    w_last(0)
    arrive(w5[0])
    wh, wl = split(jnp.concatenate([wo[0, 0], wo[0, 1]], 0))
    cpl = dot3(xh[:256, :256], xl[:256, :256], wh, wl)
    cpl_ref[0:256] = cpl
    ch, cl = split(cpl)
    for b in range(4):
        rows = slice(b * 256, b * 256 + 256)
        p_ref[rows] = t_ref[rows] - dot3(*qa[b], ch, cl)
    w_last(1)
    lower = dot3(xh[256:, :256], xl[256:, :256], wh, wl)
    arrive(w5[1])
    wh, wl = split(jnp.concatenate([wo[1, 0], wo[1, 1]], 0))
    cpl_ref[256:512] = lower + dot3(xh[256:, 256:], xl[256:, 256:], wh, wl)
    for f in pending:
        f().wait_send()


def tail_kernel(p_ref, qh_ref, ql_ref, cpl_in, r_in, out_ref, cpl_out, r_out, ch, cl):
    i = pl.program_id(0)

    @pl.when(i == 0)
    def _():
        ch[...], cl[...] = split(cpl_in[256:512])

    rows = pl.ds(pl.multiple_of(i * 128, 128), 128)
    cpl_out[...] = cpl_in[rows]
    r_out[...] = r_in[rows]
    out_ref[...] = p_ref[...] - dot3(qh_ref[...], ql_ref[...], ch[...], cl[...])


def shards(panel_matrix, trailing):
    V = pl.BlockSpec(memory_space=pltpu.VMEM)
    ANY = pl.BlockSpec(memory_space=pl.ANY)
    f = lambda *s: jax.ShapeDtypeStruct(s, F32)
    h = lambda *s: jax.ShapeDtypeStruct(s, BF16)
    v = lambda *s: pltpu.VMEM(s, F32)
    vh = lambda *s: pltpu.VMEM(s, BF16)
    dma = pltpu.SemaphoreType.DMA
    r, part, qh, ql, cpl = pl.pallas_call(
        comm_kernel,
        out_shape=(f(512, 512), f(1024, 1024), h(4, 256, 256), h(4, 256, 256), f(512, 1024)),
        in_specs=[ANY, ANY],
        out_specs=(V,) * 5,
        scratch_shapes=[
            v(4, 256, 512), v(1024, 1024), vh(1024, 1024), vh(1024, 1024), v(512, 512), v(512, 512),
            v(2, 256, 128), v(2, 384, 128), v(256, 128), v(384, 128), v(256, 128), v(512, 128),
            v(3, 64, 128), v(64, 128), v(7, 8, 128), v(7, 64, 128), v(64, 128), v(3, 16, 128),
            v(4, 8, 128), v(4, 16, 128), v(2, 256, 128), v(2, 512, 128),
            v(2, 2, 128, 1024), v(2, 128, 1024), v(2, 2, 128, 1024),
            v(2, 3, 32, WP), v(2, 32, WP), v(2, 7, 8, 384),
            v(2, 7, 16, 1024 - WP), v(2, 16, 1024 - WP), v(2, 3, 8, 128),
            dma((150,)), dma((150,)), dma((2,)),
        ],
        name="reduce_and_factor",
        compiler_params=pltpu.CompilerParams(collective_id=0, has_side_effects=True, vmem_limit_bytes=48 * 2**20),
    )(panel_matrix, trailing)

    whole = lambda *s: pl.BlockSpec(s, lambda i: (0,) * len(s))
    rows = lambda *s: pl.BlockSpec(s, lambda i: (i, 0))
    block = pl.BlockSpec((None, 256, 256), lambda i: (i, 0, 0))
    projected, coupling, r = pl.pallas_call(
        tail_kernel,
        grid=(4,),
        out_shape=(f(1024, 1024), f(512, 1024), f(512, 512)),
        in_specs=[rows(256, 1024), block, block, whole(512, 1024), whole(512, 512)],
        out_specs=(rows(256, 1024), rows(128, 1024), rows(128, 512)),
        scratch_shapes=[vh(256, 1024), vh(256, 1024)],
        name="project",
        compiler_params=pltpu.CompilerParams(vmem_limit_bytes=24 * 2**20),
    )(part, qh, ql, cpl, r)
    return r, coupling, projected


def solution(mesh):
    in_specs = (P(("row", "col"), None), P("row", "col"))
    out_specs = (P(), P(None, "col"), P("row", "col"))
    return jax.shard_map(shards, mesh=mesh, in_specs=in_specs, out_specs=out_specs, check_vma=False)
```

time: 677 us -> 84.3 us (0.12); the launches traced: 667 us -> 84.1 us
  waiting for transfers between devices: 482 us -> 0 us
  other arithmetic: 120 us -> 0 us
  Pallas kernels: 0 us -> 80.2 us
  matrix products: 31.4 us -> 0 us
  between operations: 16.8 us -> 0.66 us
  local copies, waits for them, and re-layouts: 15.9 us -> 3.22 us
    psum x2 -> x0, waiting for transfers between devices: 448 us -> none  [the longest x1 262 us: shards(): gram = lax.psum(gram_part, ('row', 'col'))]
    another operation x17 -> x0, other arithmetic: 119 us -> none  [the longest x14 78.7 us: shards(): lower_factor = jnp.linalg.cholesky(gram)]
    pallas_call x0 -> x2, Pallas kernels: none -> 80.2 us  [the longest x1 75.9 us: shards(): pl.pallas_call(comm_kernel, out_shape=(f(512, 512), f(1024, 1024), h(4, 2...]
    all_gather x1 -> x0, waiting for transfers between devices: 33.7 us -> none  [shards(): basis_block = lax.all_gather(local_basis, 'col', axis=0, tiled=True)]
    dot_general x3 -> x0, matrix products: 23.8 us -> none  [the longest x2 13.5 us: contract_rows(): lax.dot_general(left, right, (((0,), (0,)), ((), ())), precision=precise,...]
    another operation x17 -> x0, local copies, waits for them, and re-layouts: 11.6 us -> none
    another operation x13 -> x0, matrix products: 7.58 us -> none  [the longest x7 5.71 us: shards(): jax.scipy.linalg.solve_triangular(lower_factor, panel_matrix.T, lower=True)]
  transfers between devices with their start and end apart: 3 -> 0, of which waited for: 3 -> 0; matrix products, arithmetic and copies ran while one was open for 0% -> 0% of each run, Pallas kernels for 0% -> 0%
where the time goes in v2:
time: 84.3 us; the launch traced here: 84.1 us
  Pallas kernels  80.2 us (95%)
  local copies, waits for them, and re-layouts  3.22 us (4%)
    pallas_call x1, Pallas kernels, shards(): pl.pallas_call(comm_kernel, out_shape=(f(512, 512), f(1024, 1024), h(4, 2...  75.9 us
    pallas_call x1, Pallas kernels, shards(): pl.pallas_call(tail_kernel, grid=(4,), out_shape=(f(1024, 1024), f(512, 1...  4.29 us
    unnamed x4, local copies, waits for them, and re-layouts  3.22 us

profile of v2, /device:TPU:1, one launch (start us, length us, event | category | flops | bytes accessed | tf_op | source)
XLA Modules:
  0.0 84.1 jit_solution(13601554345689419832)
XLA Ops:
  0.6 0.0 copy-start.1
  0.6 1.0 %copy-done.1 = f32[256,512]{1,0:T(8,128)S(1)} copy-done((f32[256,512]{1,0:T(8,128)S(1)}, f32[256,512]{1,0:T(8,128)}, u32[]{:S(2)}) %copy-start.1) | copy-done | bytes 524312
  1.7 75.9 %reduce_and_factor.1 = (f32[512,512]{1,0:T(8,128)S(1)}, f32[1024,1024]{1,0:T(8,128)}, bf16[4,256,256]{2,1,0:T(8,128)(2,1)S(1)}, bf16[4,256,256]{2,1,0:T(8,128)(2,1)S(1)}, f32[512,1024]{1,0:T(8,128)S(1)}) custom-call(f32[256,512]{1,0:T(8,128)S(1)} %copy-done.1, f32[1024,1024]{1,0:T(8,128)} %t_hbm.1), custom_call_target="tpu_custom_call" | custom-call | tf_op jit(solution)/shard_map/reduce_and_factor/pallas_call | solution.py:424
  77.6 0.0 copy-start
  77.6 2.2 %copy-done = f32[1024,1024]{1,0:T(8,128)S(1)} copy-done((f32[1024,1024]{1,0:T(8,128)S(1)}, f32[1024,1024]{1,0:T(8,128)}, u32[]{:S(2)}) %copy-start) | copy-done | bytes 4194328
  79.8 4.3 %project.1 = (f32[1024,1024]{1,0:T(8,128)}, f32[512,1024]{1,0:T(8,128)}, f32[512,512]{1,0:T(8,128)}) custom-call(f32[1024,1024]{1,0:T(8,128)S(1)} %copy-done, bf16[4,256,256]{2,1,0:T(8,128)(2,1)S(1)} %get-tuple-element.12.qh_ref, bf16[4,256,256]{2,1,0:T(8,128)(2,1)S(1)} %get-tuple-element.13.ql_ref, f32[512,1024]{1,0:T(8,128)S(1)} %get-tuple-element.14.cpl_in, ...), custom_call_target="tpu_custom_call" | custom-call | tf_op jit(solution)/shard_map/project/pallas_call | solution.py:446
Async XLA Ops:
  0.6 1.0 %copy-start.1 = (f32[256,512]{1,0:T(8,128)S(1)}, f32[256,512]{1,0:T(8,128)}, u32[]{:S(2)}) copy-start(f32[256,512]{1,0:T(8,128)} %a_hbm.1) | copy-start | bytes 1572868
  77.6 2.2 %copy-start = (f32[1024,1024]{1,0:T(8,128)S(1)}, f32[1024,1024]{1,0:T(8,128)}, u32[]{:S(2)}) copy-start(f32[1024,1024]{1,0:T(8,128)} %get-tuple-element.11.p_ref) | copy-start | bytes 12582916

commit v3 on v2

--- a/solution.py
+++ b/solution.py
@@ -14,7 +14,6 @@
 NX, NY, NZ = 4, 4, 8
 BLOCKS0 = [(0, 0), (0, 1), (0, 2), (0, 3)]
 BLOCKS1 = [(1, 1), (1, 2), (1, 3), (2, 2), (2, 3), (3, 3)]
-WP = 768
 
 
 def split(x):
@@ -38,7 +37,7 @@
     return jnp.broadcast_to(v, B8)
 
 
-def factor128(block):
+def factor128(block, halfway=None):
     n, nb = 16, 8
     sub = lax.broadcasted_iota(jnp.int32, B8, 0)
     lan = lax.broadcasted_iota(jnp.int32, B8, 1)
@@ -87,6 +86,8 @@
             S[g] = S[g] * scale
             X[g] = X[g] * scale
         if e < n:
+            if halfway is not None:
+                halfway()
             U = jnp.concatenate(S[b:e], 0)
             both = jnp.concatenate([U, jnp.concatenate(X[b:e], 0)], 1)
             up = dot_hi(U.T[8 * e :], both)
@@ -102,7 +103,7 @@
     r_ref, p_ref, qh_ref, ql_ref, cpl_ref,
     ag, t_ref, th, tl, s_ref, x_ref, gb0, gb1, gc0, gc1, ga0, ga1,
     gl10, gr10, gl20, gl11, gr11, gl21, xb0, xb1, go0, go1,
-    w_ref, wc, wo, wl1p, wr1p, wl2p, wl1q, wr1q, wl2q,
+    w_ref, wc, wo, wl1, wr1, wl2,
     send, recv, lsem,
 ):
     r = lax.axis_index("row")
@@ -125,25 +126,27 @@
     counter = [0]
     pending = []
 
-    def copies(pairs):
-        base = counter[0]
-        counter[0] += len(pairs)
-
-        def make(k, src, dst, to):
-            return lambda: pltpu.make_async_remote_copy(
+    def copies(pairs, whole):
+        k = counter[0]
+        counter[0] += 1
+        return k, pairs, whole
+
+    def start(group):
+        k, pairs, _ = group
+        for src, dst, to in pairs:
+            pltpu.make_async_remote_copy(
                 src_ref=src, dst_ref=dst, send_sem=send.at[k], recv_sem=recv.at[k], device_id=to, device_id_type=MESH
-            )
-
-        return [make(base + k, *p) for k, p in enumerate(pairs)]
-
-    def start(group):
-        for f in group:
-            f().start()
-        pending.extend(group)
+            ).start()
+        pending.append(group)
 
     def arrive(group):
-        for f in group:
-            f().wait_recv()
+        k, _, whole = group
+        pltpu.make_async_copy(whole, whole, recv.at[k]).wait()
+
+    def sent():
+        for k, _, whole in pending:
+            pltpu.make_async_copy(whole, whole, send.at[k]).wait()
+        pending.clear()
 
     def rows_of(n):
         return lambda i: (pl.ds(pl.multiple_of(i * n, 8), n), slice(None))
@@ -153,7 +156,7 @@
 
     def scatter(axis, ref, piece, land):
         n, i, at = axes[axis]
-        return copies([(ref.at[piece((i + d) % n)], land.at[d - 1], at(d)) for d in range(1, n)])
+        return copies([(ref.at[piece((i + d) % n)], land.at[d - 1], at(d)) for d in range(1, n)], land)
 
     def summed(axis, ref, piece, land):
         n, i, _ = axes[axis]
@@ -162,9 +165,9 @@
             total = total + land[d]
         return total
 
-    def gather(axis, ref, piece):
+    def gather(axis, ref, piece, land):
         n, i, at = axes[axis]
-        return copies([(ref.at[piece(i)], ref.at[piece(i)], at(d)) for d in range(1, n)])
+        return copies([(ref.at[piece(i)], ref.at[piece(i)], at(d)) for d in range(1, n)], land)
 
     barrier = pltpu.get_barrier_semaphore()
     peers = [sibling] + [at_y(d) for d in range(1, NY)] + [at_z(d) for d in range(1, NZ)] + [at_x(d) for d in range(1, NX)]
@@ -191,21 +194,21 @@
 
     pl.semaphore_wait(barrier, len(peers))
 
-    g0_c = copies([(gb0.at[1 - c], gc0, sibling)])
-    g1_c = copies([(gb1.at[1 - c], gc1, sibling)])
+    g0_c = copies([(gb0.at[1 - c], gc0, sibling)], gc0)
+    g1_c = copies([(gb1.at[1 - c], gc1, sibling)], gc1)
     start(g0_c)
     start(g1_c)
     left, right, opposite = (x + NX - 1) % NX, (x + 1) % NX, (x + 2) % NX
     half = [slice(0, 256), slice(256, 512)]
     a1 = [
-        copies([(ag.at[x, :, half[k]], ag.at[x, :, half[k]], at_x(1)), (ag.at[x, :, half[k]], ag.at[x, :, half[k]], at_x(NX - 1))])
+        copies([(ag.at[x, :, half[k]], ag.at[x, :, half[k]], at_x(d)) for d in (1, NX - 1)], ag.at[0])
         for k in range(2)
     ]
     a2 = [
         copies([
             (ag.at[left, 0:128, half[k]], ag.at[left, 0:128, half[k]], at_x(1)),
             (ag.at[right, 128:256, half[k]], ag.at[right, 128:256, half[k]], at_x(NX - 1)),
-        ])
+        ], ag.at[0, 0:128])
         for k in range(2)
     ]
     start(a1[0])
@@ -221,37 +224,32 @@
                 part = v[m * 128 : m * 128 + 128]
                 w_ref[k, m, :, cols] = part if first else w_ref[k, m, :, cols] + part
 
-    s10 = scatter("y", ga0, rows_of(64), gl10)
-    s20 = scatter("z", gr10, rows_of(8), gl20)
-    s11 = scatter("z", ga1, rows_of(64), gl11)
-    s21 = scatter("y", gr11, rows_of(16), gl21)
-    x0 = copies([(xb0.at[x], xb0.at[x], at_x(d)) for d in range(1, NX)])
-    x1 = copies([(xb1.at[x], xb1.at[x], at_x(d)) for d in range(1, NX)])
-    o20 = gather("z", go0.at[c], lambda i: (pl.ds(pl.multiple_of(y * 64 + i * 8, 8), 8), slice(None)))
-    o10 = gather("y", go0.at[c], rows_of(64))
-    o21 = gather("y", go1.at[c], lambda i: (pl.ds(pl.multiple_of(z * 64 + i * 16, 8), 16), slice(None)))
-    o11 = gather("z", go1.at[c], rows_of(64))
-    o_c0 = copies([(go0.at[c], go0.at[c], sibling)])
-    o_c1 = copies([(go1.at[c, 0:384], go1.at[c, 0:384], sibling)])
-
-    zp, zq = halves_of(384), halves_of(128)
+    s10 = scatter("z", ga0, rows_of(32), gl10)
+    s20 = scatter("y", gr10, rows_of(8), gl20)
+    s11 = scatter("y", ga1, rows_of(128), gl11)
+    s21 = scatter("z", gr11, rows_of(16), gl21)
+    x0 = copies([(xb0.at[x], xb0.at[x], at_x(d)) for d in range(1, NX)], xb0.at[0:3])
+    x1 = copies([(xb1.at[x], xb1.at[x], at_x(d)) for d in range(1, NX)], xb1.at[0:3])
+    o20 = gather("y", go0.at[c], lambda i: (pl.ds(pl.multiple_of(z * 32 + i * 8, 8), 8), slice(None)), gl20)
+    o10 = gather("z", go0.at[c], rows_of(32), gl10)
+    o21 = gather("z", go1.at[c], lambda i: (pl.ds(pl.multiple_of(y * 128 + i * 16, 8), 16), slice(None)), gl21)
+    o11 = gather("y", go1.at[c], rows_of(128), gl11)
+    o_c0 = copies([(go0.at[c], go0.at[c], sibling)], go0.at[c])
+    o_c1 = copies([(go1.at[c, 0:384], go1.at[c, 0:384], sibling)], go1.at[c, 0:384])
+
+    zpiece = halves_of(512)
     wk = [w_ref.at[k, c] for k in range(2)]
     ok = [wo.at[k, c] for k in range(2)]
-    wp, wq = [f.at[:, 0:WP] for f in wk], [f.at[:, WP:1024] for f in wk]
-    op, oq = [f.at[:, 0:WP] for f in ok], [f.at[:, WP:1024] for f in ok]
-    w_c = [copies([(w_ref.at[k, 1 - c], wc.at[k], sibling)]) for k in range(2)]
-    w1 = [scatter("y", wp[k], rows_of(32), wl1p.at[k]) + scatter("z", wq[k], rows_of(16), wl1q.at[k]) for k in range(2)]
-    w2 = [scatter("z", wr1p.at[k], zp, wl2p.at[k]) + scatter("y", wr1q.at[k], zq, wl2q.at[k]) for k in range(2)]
-
-    def piece_p(i):
-        return (pl.ds(pl.multiple_of(y * 32 + i // 2 * 8, 8), 8), pl.ds(pl.multiple_of(i % 2 * 384, 128), 384))
-
-    def piece_q(i):
-        return (pl.ds(pl.multiple_of(z * 16 + i // 2 * 8, 8), 8), pl.ds(pl.multiple_of(i % 2 * 128, 128), 128))
-
-    w3 = [gather("z", op[k], piece_p) + gather("y", oq[k], piece_q) for k in range(2)]
-    w4 = [gather("y", op[k], rows_of(32)) + gather("z", oq[k], rows_of(16)) for k in range(2)]
-    w5 = [copies([(ok[k], ok[k], sibling)]) for k in range(2)]
+
+    def in_y(i):
+        return (pl.ds(pl.multiple_of(y * 32 + i // 2 * 8, 8), 8), pl.ds(pl.multiple_of(i % 2 * 512, 128), 512))
+
+    w_c = [copies([(w_ref.at[k, 1 - c], wc.at[k], sibling)], wc.at[k]) for k in range(2)]
+    w1 = [scatter("y", wk[k], rows_of(32), wl1.at[k]) for k in range(2)]
+    w2 = [scatter("z", wr1.at[k], zpiece, wl2.at[k]) for k in range(2)]
+    w3 = [gather("z", ok[k], in_y, wl2.at[k]) for k in range(2)]
+    w4 = [gather("y", ok[k], rows_of(32), wl1.at[k]) for k in range(2)]
+    w5 = [copies([(ok[k], ok[k], sibling)], ok[k]) for k in range(2)]
 
     def w_core(k):
         arrive(w_c[k])
@@ -260,14 +258,12 @@
 
     def w_first(k):
         arrive(w1[k])
-        wr1p[k] = summed("y", wp[k], rows_of(32), wl1p.at[k])
-        wr1q[k] = summed("z", wq[k], rows_of(16), wl1q.at[k])
+        wr1[k] = summed("y", wk[k], rows_of(32), wl1.at[k])
         start(w2[k])
 
     def w_second(k):
         arrive(w2[k])
-        op[k][piece_p(z)] = summed("z", wr1p.at[k], zp, wl2p.at[k])
-        oq[k][piece_q(y)] = summed("y", wr1q.at[k], zq, wl2q.at[k])
+        ok[k][in_y(z)] = summed("z", wr1.at[k], zpiece, wl2.at[k])
         start(w3[k])
 
     def w_third(k):
@@ -291,28 +287,28 @@
     w_block(x, 0, True)
 
     arrive(s10)
-    gr10[...] = summed("y", ga0, rows_of(64), gl10)
+    gr10[...] = summed("z", ga0, rows_of(32), gl10)
     start(s20)
     arrive(s11)
-    gr11[...] = summed("z", ga1, rows_of(64), gl11)
+    gr11[...] = summed("y", ga1, rows_of(128), gl11)
     start(s21)
     arrive(a1[0])
     start(a2[0])
     w_block(left, 0)
     arrive(s20)
-    xb0[x] = summed("z", gr10, rows_of(8), gl20)
+    xb0[x] = summed("y", gr10, rows_of(8), gl20)
     start(x0)
     arrive(s21)
-    xb1[x] = summed("y", gr11, rows_of(16), gl21)
+    xb1[x] = summed("z", gr11, rows_of(16), gl21)
     start(x1)
     w_block(right, 0)
     arrive(a1[1])
     start(a2[1])
     arrive(x0)
-    go0[c, pl.ds(pl.multiple_of(y * 64 + z * 8, 8), 8), :] = (xb0[0] + xb0[1]) + (xb0[2] + xb0[3])
+    go0[c, pl.ds(pl.multiple_of(z * 32 + y * 8, 8), 8), :] = (xb0[0] + xb0[1]) + (xb0[2] + xb0[3])
     start(o20)
     arrive(x1)
-    go1[c, pl.ds(pl.multiple_of(z * 64 + y * 16, 8), 16), :] = (xb1[0] + xb1[1]) + (xb1[2] + xb1[3])
+    go1[c, pl.ds(pl.multiple_of(y * 128 + z * 16, 8), 16), :] = (xb1[0] + xb1[1]) + (xb1[2] + xb1[3])
     start(o21)
     arrive(a2[0])
     w_block(opposite, 0)
@@ -342,19 +338,17 @@
     diag = s_ref[0:128, 0:128]
     for J in range(4):
         a, b, q = J * 128, J * 128 + 128, J * 128 + 256
-        r11, li = factor128(diag)
+        if J == 0:
+            w_first(0)
+        r11, li = factor128(diag, {1: lambda: w_first(1), 2: lambda: w_third(0)}.get(J))
         r_ref[a:b, a:b] = r11
         x_ref[a:b, a:b] = li
         if J == 0:
             arrive(o_c1)
             for n, (i, j) in enumerate(BLOCKS1):
                 s_ref[i * 128 : i * 128 + 128, j * 128 : j * 128 + 128] = go1[n // 3, n % 3 * 128 : n % 3 * 128 + 128, :]
-            w_first(0)
-        if J == 1:
-            w_first(1)
             w_second(0)
         if J == 2:
-            w_third(0)
             w_second(1)
         if J < 3:
             r12 = dot_hi(li, s_ref[a:b, b:q])
@@ -369,7 +363,6 @@
             x_ref[a:b, :a] = dot_hi(li, x_ref[a:b, :a])
         if J < 3:
             x_ref[b:, :b] = x_ref[b:, :b] - dot_hi(r_ref[a:b, b:].T, x_ref[a:b, :b])
-    w_third(1)
 
     xi = x_ref[...]
     xh, xl = split(xi)
@@ -382,6 +375,7 @@
     qa = [basis(b, half[0]) for b in range(4)]
     for b in range(4):
         qh_ref[b], ql_ref[b] = basis(b, half[1])
+    w_third(1)
     w_last(0)
     arrive(w5[0])
     wh, wl = split(jnp.concatenate([wo[0, 0], wo[0, 1]], 0))
@@ -396,8 +390,7 @@
     arrive(w5[1])
     wh, wl = split(jnp.concatenate([wo[1, 0], wo[1, 1]], 0))
     cpl_ref[256:512] = lower + dot3(xh[256:, 256:], xl[256:, 256:], wh, wl)
-    for f in pending:
-        f().wait_send()
+    sent()
 
 
 def tail_kernel(p_ref, qh_ref, ql_ref, cpl_in, r_in, out_ref, cpl_out, r_out, ch, cl):
@@ -415,7 +408,7 @@
 
 def shards(panel_matrix, trailing):
     V = pl.BlockSpec(memory_space=pltpu.VMEM)
-    ANY = pl.BlockSpec(memory_space=pl.ANY)
+    HBM = pl.BlockSpec(memory_space=pltpu.HBM)
     f = lambda *s: jax.ShapeDtypeStruct(s, F32)
     h = lambda *s: jax.ShapeDtypeStruct(s, BF16)
     v = lambda *s: pltpu.VMEM(s, F32)
@@ -424,20 +417,19 @@
     r, part, qh, ql, cpl = pl.pallas_call(
         comm_kernel,
         out_shape=(f(512, 512), f(1024, 1024), h(4, 256, 256), h(4, 256, 256), f(512, 1024)),
-        in_specs=[ANY, ANY],
+        in_specs=[HBM, HBM],
         out_specs=(V,) * 5,
         scratch_shapes=[
             v(4, 256, 512), v(1024, 1024), vh(1024, 1024), vh(1024, 1024), v(512, 512), v(512, 512),
             v(2, 256, 128), v(2, 384, 128), v(256, 128), v(384, 128), v(256, 128), v(512, 128),
-            v(3, 64, 128), v(64, 128), v(7, 8, 128), v(7, 64, 128), v(64, 128), v(3, 16, 128),
+            v(7, 32, 128), v(32, 128), v(3, 8, 128), v(3, 128, 128), v(128, 128), v(7, 16, 128),
             v(4, 8, 128), v(4, 16, 128), v(2, 256, 128), v(2, 512, 128),
             v(2, 2, 128, 1024), v(2, 128, 1024), v(2, 2, 128, 1024),
-            v(2, 3, 32, WP), v(2, 32, WP), v(2, 7, 8, 384),
-            v(2, 7, 16, 1024 - WP), v(2, 16, 1024 - WP), v(2, 3, 8, 128),
-            dma((150,)), dma((150,)), dma((2,)),
+            v(2, 3, 32, 1024), v(2, 32, 1024), v(2, 7, 8, 512),
+            dma((40,)), dma((40,)), dma((2,)),
         ],
         name="reduce_and_factor",
-        compiler_params=pltpu.CompilerParams(collective_id=0, has_side_effects=True, vmem_limit_bytes=48 * 2**20),
+        compiler_params=pltpu.CompilerParams(collective_id=0, has_side_effects=True, vmem_limit_bytes=45 * 2**20),
     )(panel_matrix, trailing)
 
     whole = lambda *s: pl.BlockSpec(s, lambda i: (0,) * len(s))

time: 84.3 us -> 77.4 us (0.918)
  Pallas kernels: 80.2 us -> 75.6 us
  local copies, waits for them, and re-layouts: 3.22 us -> 1.03 us
    pallas_call x1, Pallas kernels: 75.9 us -> 71.3 us  [shards(): pl.pallas_call(comm_kernel, out_shape=(f(512, 512), f(1024, 1024), h(4, 2...]
    unnamed x4 -> x2, local copies, waits for them, and re-layouts: 3.22 us -> 1.03 us
where the time goes in v3:
time: 77.4 us; the launch traced here: 77.3 us
  Pallas kernels  75.6 us (98%)
  local copies, waits for them, and re-layouts  1.03 us (1%)
    pallas_call x1, Pallas kernels, shards(): pl.pallas_call(comm_kernel, out_shape=(f(512, 512), f(1024, 1024), h(4, 2...  71.3 us
    pallas_call x1, Pallas kernels, shards(): pl.pallas_call(tail_kernel, grid=(4,), out_shape=(f(1024, 1024), f(512, 1...  4.33 us

profile of v3, /device:TPU:1, one launch (start us, length us, event | category | flops | bytes accessed | tf_op | source)
XLA Modules:
  0.0 77.3 jit_solution(5752855941954190429)
XLA Ops:
  0.6 0.0 copy-start
  0.6 1.0 %copy-done = f32[256,512]{1,0:T(8,128)S(1)} copy-done((f32[256,512]{1,0:T(8,128)S(1)}, f32[256,512]{1,0:T(8,128)}, u32[]{:S(2)}) %copy-start) | copy-done | bytes 524312
  1.7 71.3 %reduce_and_factor.1 = (f32[512,512]{1,0:T(8,128)S(1)}, f32[1024,1024]{1,0:T(8,128)S(1)}, bf16[4,256,256]{2,1,0:T(8,128)(2,1)S(1)}, bf16[4,256,256]{2,1,0:T(8,128)(2,1)S(1)}, f32[512,1024]{1,0:T(8,128)S(1)}) custom-call(f32[256,512]{1,0:T(8,128)S(1)} %copy-done, f32[1024,1024]{1,0:T(8,128)} %t_hbm.1), custom_call_target="tpu_custom_call" | custom-call | tf_op jit(solution)/shard_map/reduce_and_factor/pallas_call | solution.py:417
  72.9 4.3 %project.1 = (f32[1024,1024]{1,0:T(8,128)}, f32[512,1024]{1,0:T(8,128)}, f32[512,512]{1,0:T(8,128)}) custom-call(f32[1024,1024]{1,0:T(8,128)S(1)} %get-tuple-element.11.p_ref, bf16[4,256,256]{2,1,0:T(8,128)(2,1)S(1)} %get-tuple-element.12.qh_ref, bf16[4,256,256]{2,1,0:T(8,128)(2,1)S(1)} %get-tuple-element.13.ql_ref, ...), custom_call_target="tpu_custom_call" | custom-call | tf_op jit(solution)/shard_map/project/pallas_call | solution.py:438
Async XLA Ops:
  0.6 1.0 %copy-start = (f32[256,512]{1,0:T(8,128)S(1)}, f32[256,512]{1,0:T(8,128)}, u32[]{:S(2)}) copy-start(f32[256,512]{1,0:T(8,128)} %a_hbm.1) | copy-start | bytes 1572868

commit v4 on v3

--- a/solution.py
+++ b/solution.py
@@ -151,9 +151,6 @@
     def rows_of(n):
         return lambda i: (pl.ds(pl.multiple_of(i * n, 8), n), slice(None))
 
-    def halves_of(cols):
-        return lambda i: (pl.ds(pl.multiple_of(i // 2 * 8, 8), 8), pl.ds(pl.multiple_of(i % 2 * cols, 128), cols))
-
     def scatter(axis, ref, piece, land):
         n, i, at = axes[axis]
         return copies([(ref.at[piece((i + d) % n)], land.at[d - 1], at(d)) for d in range(1, n)], land)
@@ -199,30 +196,31 @@
     start(g0_c)
     start(g1_c)
     left, right, opposite = (x + NX - 1) % NX, (x + 1) % NX, (x + 2) % NX
-    half = [slice(0, 256), slice(256, 512)]
+    part = [slice(128 * k, 128 * k + 128) for k in range(4)]
     a1 = [
-        copies([(ag.at[x, :, half[k]], ag.at[x, :, half[k]], at_x(d)) for d in (1, NX - 1)], ag.at[0])
-        for k in range(2)
+        copies([(ag.at[x, :, part[k]], ag.at[x, :, part[k]], at_x(d)) for d in (1, NX - 1)], ag.at[0, 0:128])
+        for k in range(4)
     ]
     a2 = [
         copies([
-            (ag.at[left, 0:128, half[k]], ag.at[left, 0:128, half[k]], at_x(1)),
-            (ag.at[right, 128:256, half[k]], ag.at[right, 128:256, half[k]], at_x(NX - 1)),
-        ], ag.at[0, 0:128])
-        for k in range(2)
+            (ag.at[left, 0:128, part[k]], ag.at[left, 0:128, part[k]], at_x(1)),
+            (ag.at[right, 128:256, part[k]], ag.at[right, 128:256, part[k]], at_x(NX - 1)),
+        ], ag.at[0, 0:64])
+        for k in range(4)
     ]
-    start(a1[0])
-    start(a1[1])
-
-    def w_block(b, k, first=False):
-        ah, al = split(ag[b, :, half[k]].T)
+    for k in range(4):
+        start(a1[k])
+
+    def w_block(b, k, n, first=False):
+        ah, al = split(ag[b, :, 128 * k : 128 * (k + n)].T)
         rows = pl.ds(pl.multiple_of(b * 256, 256), 256)
-        for n in range(4):
-            cols = slice(n * 256, n * 256 + 256)
+        for q in range(4):
+            cols = slice(q * 256, q * 256 + 256)
             v = dot3(ah, al, th[rows, cols], tl[rows, cols])
-            for m in range(2):
-                part = v[m * 128 : m * 128 + 128]
-                w_ref[k, m, :, cols] = part if first else w_ref[k, m, :, cols] + part
+            for m in range(2 * n):
+                part_m = v[m * 64 : m * 64 + 64]
+                k_m = k + m // 2
+                w_ref[k_m, m % 2, :, cols] = part_m if first else w_ref[k_m, m % 2, :, cols] + part_m
 
     s10 = scatter("z", ga0, rows_of(32), gl10)
     s20 = scatter("y", gr10, rows_of(8), gl20)
@@ -237,19 +235,24 @@
     o_c0 = copies([(go0.at[c], go0.at[c], sibling)], go0.at[c])
     o_c1 = copies([(go1.at[c, 0:384], go1.at[c, 0:384], sibling)], go1.at[c, 0:384])
 
-    zpiece = halves_of(512)
-    wk = [w_ref.at[k, c] for k in range(2)]
-    ok = [wo.at[k, c] for k in range(2)]
+    wk = [w_ref.at[k, c] for k in range(4)]
+    ok = [wo.at[k, c] for k in range(4)]
+
+    def quarter(i, first_row=0):
+        return (
+            pl.ds(pl.multiple_of(first_row + i // 4 * 8, 8), 8),
+            pl.ds(pl.multiple_of(i % 4 * 256, 128), 256),
+        )
 
     def in_y(i):
-        return (pl.ds(pl.multiple_of(y * 32 + i // 2 * 8, 8), 8), pl.ds(pl.multiple_of(i % 2 * 512, 128), 512))
-
-    w_c = [copies([(w_ref.at[k, 1 - c], wc.at[k], sibling)], wc.at[k]) for k in range(2)]
-    w1 = [scatter("y", wk[k], rows_of(32), wl1.at[k]) for k in range(2)]
-    w2 = [scatter("z", wr1.at[k], zpiece, wl2.at[k]) for k in range(2)]
-    w3 = [gather("z", ok[k], in_y, wl2.at[k]) for k in range(2)]
-    w4 = [gather("y", ok[k], rows_of(32), wl1.at[k]) for k in range(2)]
-    w5 = [copies([(ok[k], ok[k], sibling)], ok[k]) for k in range(2)]
+        return quarter(i, y * 16)
+
+    w_c = [copies([(w_ref.at[k, 1 - c], wc.at[k], sibling)], wc.at[k]) for k in range(4)]
+    w1 = [scatter("y", wk[k], rows_of(16), wl1.at[k]) for k in range(4)]
+    w2 = [scatter("z", wr1.at[k], quarter, wl2.at[k]) for k in range(4)]
+    w3 = [gather("z", ok[k], in_y, wl2.at[k]) for k in range(4)]
+    w4 = [gather("y", ok[k], rows_of(16), wl1.at[k]) for k in range(4)]
+    w5 = [copies([(ok[k], ok[k], sibling)], ok[k]) for k in range(4)]
 
     def w_core(k):
         arrive(w_c[k])
@@ -258,12 +261,12 @@
 
     def w_first(k):
         arrive(w1[k])
-        wr1[k] = summed("y", wk[k], rows_of(32), wl1.at[k])
+        wr1[k] = summed("y", wk[k], rows_of(16), wl1.at[k])
         start(w2[k])
 
     def w_second(k):
         arrive(w2[k])
-        ok[k][in_y(z)] = summed("z", wr1.at[k], zpiece, wl2.at[k])
+        ok[k][in_y(z)] = summed("z", wr1.at[k], quarter, wl2.at[k])
         start(w3[k])
 
     def w_third(k):
@@ -284,72 +287,103 @@
 
     load_t.wait()
     th[...], tl[...] = split(t_ref[...])
-    w_block(x, 0, True)
-
+    w_block(x, 0, 4, True)
+
+    def pass_on(k):
+        arrive(a1[k])
+        start(a2[k])
+
+    def opposite_block(k):
+        arrive(a2[k])
+        w_block(opposite, k, 1)
+        start(w_c[k])
+
+    pass_on(0)
     arrive(s10)
     gr10[...] = summed("z", ga0, rows_of(32), gl10)
     start(s20)
     arrive(s11)
     gr11[...] = summed("y", ga1, rows_of(128), gl11)
     start(s21)
-    arrive(a1[0])
-    start(a2[0])
-    w_block(left, 0)
+    pass_on(1)
+    w_block(left, 0, 2)
+    w_block(right, 0, 2)
+    pass_on(2)
     arrive(s20)
     xb0[x] = summed("y", gr10, rows_of(8), gl20)
     start(x0)
     arrive(s21)
     xb1[x] = summed("z", gr11, rows_of(16), gl21)
     start(x1)
-    w_block(right, 0)
-    arrive(a1[1])
-    start(a2[1])
+    opposite_block(0)
+    pass_on(3)
+    w_block(left, 2, 2)
+    w_block(right, 2, 2)
+    w_core(0)
+    opposite_block(1)
     arrive(x0)
     go0[c, pl.ds(pl.multiple_of(z * 32 + y * 8, 8), 8), :] = (xb0[0] + xb0[1]) + (xb0[2] + xb0[3])
     start(o20)
     arrive(x1)
     go1[c, pl.ds(pl.multiple_of(y * 128 + z * 16, 8), 16), :] = (xb1[0] + xb1[1]) + (xb1[2] + xb1[3])
     start(o21)
-    arrive(a2[0])
-    w_block(opposite, 0)
-    start(w_c[0])
-    w_block(x, 1, True)
+    w_core(1)
+    opposite_block(2)
+    w_core(2)
     arrive(o20)
     start(o10)
+    opposite_block(3)
+    w_first(0)
     arrive(o21)
     start(o11)
-    w_core(0)
-    w_block(left, 1)
-    w_block(right, 1)
+    w_core(3)
+    w_first(1)
+    r_ref[...] = jnp.zeros_like(r_ref)
+    x_ref[...] = jnp.zeros_like(x_ref)
     arrive(o10)
     start(o_c0)
-    arrive(a2[1])
-    w_block(opposite, 1)
-    start(w_c[1])
+    w_first(2)
     arrive(o_c0)
     for n, (i, j) in enumerate(BLOCKS0):
         s_ref[:128, j * 128 : j * 128 + 128] = go0[n // 2, n % 2 * 128 : n % 2 * 128 + 128, :]
-    r_ref[...] = jnp.zeros_like(r_ref)
-    x_ref[...] = jnp.zeros_like(x_ref)
     arrive(o11)
     start(o_c1)
-    w_core(1)
+    w_second(0)
+
+    def at_half(J):
+        if J == 0:
+            w_first(3)
+            w_second(1)
+        if J == 1:
+            w_third(0)
+            w_second(3)
+        if J == 2:
+            w_third(2)
+        if J == 3:
+            w_last(1)
+
+    def at_end(J):
+        if J == 0:
+            w_second(2)
+        if J == 1:
+            w_third(1)
+        if J == 2:
+            w_third(3)
+            w_last(0)
+        if J == 3:
+            w_last(2)
 
     diag = s_ref[0:128, 0:128]
     for J in range(4):
         a, b, q = J * 128, J * 128 + 128, J * 128 + 256
-        if J == 0:
-            w_first(0)
-        r11, li = factor128(diag, {1: lambda: w_first(1), 2: lambda: w_third(0)}.get(J))
+        r11, li = factor128(diag, lambda: at_half(J))
         r_ref[a:b, a:b] = r11
         x_ref[a:b, a:b] = li
         if J == 0:
             arrive(o_c1)
             for n, (i, j) in enumerate(BLOCKS1):
                 s_ref[i * 128 : i * 128 + 128, j * 128 : j * 128 + 128] = go1[n // 3, n % 3 * 128 : n % 3 * 128 + 128, :]
-            w_second(0)
-        if J == 2:
-            w_second(1)
+        at_end(J)
         if J < 3:
             r12 = dot_hi(li, s_ref[a:b, b:q])
             r_ref[a:b, b:q] = r12
@@ -372,24 +406,28 @@
         ah, al = split(ag[rows][:, : cols.stop])
         return split(dot3(ah, al, xth[: cols.stop, cols], xtl[: cols.stop, cols]))
 
-    qa = [basis(b, half[0]) for b in range(4)]
+    most, last = slice(0, 384), slice(384, 512)
+    qa = [basis(b, most) for b in range(4)]
     for b in range(4):
-        qh_ref[b], ql_ref[b] = basis(b, half[1])
-    w_third(1)
-    w_last(0)
+        qh_ref[b], ql_ref[b] = basis(b, last)
     arrive(w5[0])
-    wh, wl = split(jnp.concatenate([wo[0, 0], wo[0, 1]], 0))
-    cpl = dot3(xh[:256, :256], xl[:256, :256], wh, wl)
-    cpl_ref[0:256] = cpl
-    ch, cl = split(cpl)
+    arrive(w5[1])
+    wh, wl = split(wo[0:2].reshape(256, 1024))
+    cpl_a = dot3(xh[:256, :256], xl[:256, :256], wh, wl)
+    cpl_b = dot3(xh[256:, :256], xl[256:, :256], wh, wl)
+    cpl_ref[0:256] = cpl_a
+    w_last(3)
+    arrive(w5[2])
+    wh, wl = split(wo[2].reshape(128, 1024))
+    cpl_b = cpl_b + dot3(xh[256:, 256:384], xl[256:, 256:384], wh, wl)
+    cpl_ref[256:384] = cpl_b[:128]
+    ch, cl = split(jnp.concatenate([cpl_a, cpl_b[:128]], 0))
     for b in range(4):
         rows = slice(b * 256, b * 256 + 256)
         p_ref[rows] = t_ref[rows] - dot3(*qa[b], ch, cl)
-    w_last(1)
-    lower = dot3(xh[256:, :256], xl[256:, :256], wh, wl)
-    arrive(w5[1])
-    wh, wl = split(jnp.concatenate([wo[1, 0], wo[1, 1]], 0))
-    cpl_ref[256:512] = lower + dot3(xh[256:, 256:], xl[256:, 256:], wh, wl)
+    arrive(w5[3])
+    wh, wl = split(wo[3].reshape(128, 1024))
+    cpl_ref[384:512] = cpl_b[128:] + dot3(xh[384:, 384:], xl[384:, 384:], wh, wl)
     sent()
 
 
@@ -398,7 +436,7 @@
 
     @pl.when(i == 0)
     def _():
-        ch[...], cl[...] = split(cpl_in[256:512])
+        ch[...], cl[...] = split(cpl_in[384:512])
 
     rows = pl.ds(pl.multiple_of(i * 128, 128), 128)
     cpl_out[...] = cpl_in[rows]
@@ -416,7 +454,7 @@
     dma = pltpu.SemaphoreType.DMA
     r, part, qh, ql, cpl = pl.pallas_call(
         comm_kernel,
-        out_shape=(f(512, 512), f(1024, 1024), h(4, 256, 256), h(4, 256, 256), f(512, 1024)),
+        out_shape=(f(512, 512), f(1024, 1024), h(4, 256, 128), h(4, 256, 128), f(512, 1024)),
         in_specs=[HBM, HBM],
         out_specs=(V,) * 5,
         scratch_shapes=[
@@ -424,9 +462,9 @@
             v(2, 256, 128), v(2, 384, 128), v(256, 128), v(384, 128), v(256, 128), v(512, 128),
             v(7, 32, 128), v(32, 128), v(3, 8, 128), v(3, 128, 128), v(128, 128), v(7, 16, 128),
             v(4, 8, 128), v(4, 16, 128), v(2, 256, 128), v(2, 512, 128),
-            v(2, 2, 128, 1024), v(2, 128, 1024), v(2, 2, 128, 1024),
-            v(2, 3, 32, 1024), v(2, 32, 1024), v(2, 7, 8, 512),
-            dma((40,)), dma((40,)), dma((2,)),
+            v(4, 2, 64, 1024), v(4, 64, 1024), v(4, 2, 64, 1024),
+            v(4, 3, 16, 1024), v(4, 16, 1024), v(4, 7, 8, 256),
+            dma((48,)), dma((48,)), dma((2,)),
         ],
         name="reduce_and_factor",
         compiler_params=pltpu.CompilerParams(collective_id=0, has_side_effects=True, vmem_limit_bytes=45 * 2**20),
@@ -434,14 +472,14 @@
 
     whole = lambda *s: pl.BlockSpec(s, lambda i: (0,) * len(s))
     rows = lambda *s: pl.BlockSpec(s, lambda i: (i, 0))
-    block = pl.BlockSpec((None, 256, 256), lambda i: (i, 0, 0))
+    block = pl.BlockSpec((None, 256, 128), lambda i: (i, 0, 0))
     projected, coupling, r = pl.pallas_call(
         tail_kernel,
         grid=(4,),
         out_shape=(f(1024, 1024), f(512, 1024), f(512, 512)),
         in_specs=[rows(256, 1024), block, block, whole(512, 1024), whole(512, 512)],
         out_specs=(rows(256, 1024), rows(128, 1024), rows(128, 512)),
-        scratch_shapes=[vh(256, 1024), vh(256, 1024)],
+        scratch_shapes=[vh(128, 1024), vh(128, 1024)],
         name="project",
         compiler_params=pltpu.CompilerParams(vmem_limit_bytes=24 * 2**20),
     )(part, qh, ql, cpl, r)

time: 77.4 us -> 73.3 us (0.947)
  Pallas kernels: 75.6 us -> 71.5 us
    pallas_call x1, Pallas kernels: 71.3 us -> 67.3 us  [shards(): pl.pallas_call(comm_kernel, out_shape=(f(512, 512), f(1024, 1024), h(4, 2...]
where the time goes in v4:
time: 73.3 us; the launch traced here: 73.2 us
  Pallas kernels  71.5 us (98%)
  local copies, waits for them, and re-layouts  1.03 us (1%)
    pallas_call x1, Pallas kernels, shards(): pl.pallas_call(comm_kernel, out_shape=(f(512, 512), f(1024, 1024), h(4, 2...  67.3 us
    pallas_call x1, Pallas kernels, shards(): pl.pallas_call(tail_kernel, grid=(4,), out_shape=(f(1024, 1024), f(512, 1...  4.22 us

profile of v4, /device:TPU:1, one launch (start us, length us, event | category | flops | bytes accessed | tf_op | source)
XLA Modules:
  0.0 73.2 jit_solution(1983051860415722615)
XLA Ops:
  0.6 0.0 copy-start
  0.6 1.0 %copy-done = f32[256,512]{1,0:T(8,128)S(1)} copy-done((f32[256,512]{1,0:T(8,128)S(1)}, f32[256,512]{1,0:T(8,128)}, u32[]{:S(2)}) %copy-start) | copy-done | bytes 524312
  1.7 67.3 %reduce_and_factor.1 = (f32[512,512]{1,0:T(8,128)S(1)}, f32[1024,1024]{1,0:T(8,128)S(1)}, bf16[4,256,128]{2,1,0:T(8,128)(2,1)S(1)}, bf16[4,256,128]{2,1,0:T(8,128)(2,1)S(1)}, f32[512,1024]{1,0:T(8,128)S(1)}) custom-call(f32[256,512]{1,0:T(8,128)S(1)} %copy-done, f32[1024,1024]{1,0:T(8,128)} %t_hbm.1), custom_call_target="tpu_custom_call" | custom-call | tf_op jit(solution)/shard_map/reduce_and_factor/pallas_call | solution.py:455
  69.0 4.2 %project.1 = (f32[1024,1024]{1,0:T(8,128)}, f32[512,1024]{1,0:T(8,128)}, f32[512,512]{1,0:T(8,128)}) custom-call(f32[1024,1024]{1,0:T(8,128)S(1)} %get-tuple-element.11.p_ref, bf16[4,256,128]{2,1,0:T(8,128)(2,1)S(1)} %get-tuple-element.12.qh_ref, bf16[4,256,128]{2,1,0:T(8,128)(2,1)S(1)} %get-tuple-element.13.ql_ref, ...), custom_call_target="tpu_custom_call" | custom-call | tf_op jit(solution)/shard_map/project/pallas_call | solution.py:476
Async XLA Ops:
  0.6 1.0 %copy-start = (f32[256,512]{1,0:T(8,128)S(1)}, f32[256,512]{1,0:T(8,128)}, u32[]{:S(2)}) copy-start(f32[256,512]{1,0:T(8,128)} %a_hbm.1) | copy-start | bytes 1572868

commit v5 on v4

--- a/solution.py
+++ b/solution.py
@@ -176,25 +176,8 @@
     load_t.start()
     load_a.wait()
 
-    a_own = ag[x]
-    a_own_t = a_own.T
-    for i in range(4):
-        rows = dot_hi(a_own_t[i * 128 : i * 128 + 128], a_own[:, i * 128 :])
-        for j in range(i, 4):
-            part = rows[:, (j - i) * 128 : (j - i) * 128 + 128]
-            if i == 0:
-                n = BLOCKS0.index((i, j))
-                gb0[n // 2, n % 2 * 128 : n % 2 * 128 + 128, :] = part
-            else:
-                n = BLOCKS1.index((i, j))
-                gb1[n // 3, n % 3 * 128 : n % 3 * 128 + 128, :] = part
-
     pl.semaphore_wait(barrier, len(peers))
 
-    g0_c = copies([(gb0.at[1 - c], gc0, sibling)], gc0)
-    g1_c = copies([(gb1.at[1 - c], gc1, sibling)], gc1)
-    start(g0_c)
-    start(g1_c)
     left, right, opposite = (x + NX - 1) % NX, (x + 1) % NX, (x + 2) % NX
     part = [slice(128 * k, 128 * k + 128) for k in range(4)]
     a1 = [
@@ -211,6 +194,24 @@
     for k in range(4):
         start(a1[k])
 
+    a_own = ag[x]
+    a_own_t = a_own.T
+    for i in range(4):
+        rows = dot_hi(a_own_t[i * 128 : i * 128 + 128], a_own[:, i * 128 :])
+        for j in range(i, 4):
+            part = rows[:, (j - i) * 128 : (j - i) * 128 + 128]
+            if i == 0:
+                n = BLOCKS0.index((i, j))
+                gb0[n // 2, n % 2 * 128 : n % 2 * 128 + 128, :] = part
+            else:
+                n = BLOCKS1.index((i, j))
+                gb1[n // 3, n % 3 * 128 : n % 3 * 128 + 128, :] = part
+
+    g0_c = copies([(gb0.at[1 - c], gc0, sibling)], gc0)
+    g1_c = copies([(gb1.at[1 - c], gc1, sibling)], gc1)
+    start(g0_c)
+    start(g1_c)
+
     def w_block(b, k, n, first=False):
         ah, al = split(ag[b, :, 128 * k : 128 * (k + n)].T)
         rows = pl.ds(pl.multiple_of(b * 256, 256), 256)
@@ -277,6 +278,15 @@
         arrive(w4[k])
         start(w5[k])
 
+    def pass_on(k):
+        arrive(a1[k])
+        start(a2[k])
+
+    def opposite_block(k):
+        arrive(a2[k])
+        w_block(opposite, k, 1)
+        start(w_c[k])
+
     arrive(g0_c)
     ga0[...] = gb0[c] + gc0[...]
     start(s10)
@@ -284,20 +294,9 @@
     ga1[0:384] = gb1[c] + gc1[...]
     ga1[384:512] = jnp.zeros((128, 128), F32)
     start(s11)
-
     load_t.wait()
     th[...], tl[...] = split(t_ref[...])
     w_block(x, 0, 4, True)
-
-    def pass_on(k):
-        arrive(a1[k])
-        start(a2[k])
-
-    def opposite_block(k):
-        arrive(a2[k])
-        w_block(opposite, k, 1)
-        start(w_c[k])
-
     pass_on(0)
     arrive(s10)
     gr10[...] = summed("z", ga0, rows_of(32), gl10)
@@ -317,10 +316,10 @@
     start(x1)
     opposite_block(0)
     pass_on(3)
+    opposite_block(1)
+    w_core(0)
     w_block(left, 2, 2)
     w_block(right, 2, 2)
-    w_core(0)
-    opposite_block(1)
     arrive(x0)
     go0[c, pl.ds(pl.multiple_of(z * 32 + y * 8, 8), 8), :] = (xb0[0] + xb0[1]) + (xb0[2] + xb0[3])
     start(o20)
@@ -329,30 +328,30 @@
     start(o21)
     w_core(1)
     opposite_block(2)
+    opposite_block(3)
     w_core(2)
+    w_first(0)
+    w_core(3)
     arrive(o20)
     start(o10)
-    opposite_block(3)
-    w_first(0)
     arrive(o21)
     start(o11)
-    w_core(3)
     w_first(1)
     r_ref[...] = jnp.zeros_like(r_ref)
     x_ref[...] = jnp.zeros_like(x_ref)
+    w_first(2)
     arrive(o10)
     start(o_c0)
-    w_first(2)
+    arrive(o11)
+    start(o_c1)
+    w_second(0)
+    w_first(3)
     arrive(o_c0)
     for n, (i, j) in enumerate(BLOCKS0):
         s_ref[:128, j * 128 : j * 128 + 128] = go0[n // 2, n % 2 * 128 : n % 2 * 128 + 128, :]
-    arrive(o11)
-    start(o_c1)
-    w_second(0)
 
     def at_half(J):
         if J == 0:
-            w_first(3)
             w_second(1)
         if J == 1:
             w_third(0)
@@ -370,8 +369,6 @@
         if J == 2:
             w_third(3)
             w_last(0)
-        if J == 3:
-            w_last(2)
 
     diag = s_ref[0:128, 0:128]
     for J in range(4):
@@ -410,6 +407,7 @@
     qa = [basis(b, most) for b in range(4)]
     for b in range(4):
         qh_ref[b], ql_ref[b] = basis(b, last)
+    w_last(2)
     arrive(w5[0])
     arrive(w5[1])
     wh, wl = split(wo[0:2].reshape(256, 1024))
@@ -441,7 +439,8 @@
     rows = pl.ds(pl.multiple_of(i * 128, 128), 128)
     cpl_out[...] = cpl_in[rows]
     r_out[...] = r_in[rows]
-    out_ref[...] = p_ref[...] - dot3(qh_ref[...], ql_ref[...], ch[...], cl[...])
+    block = pl.ds(pl.multiple_of(i * 256, 256), 256)
+    out_ref[...] = p_ref[block] - dot3(qh_ref[i], ql_ref[i], ch[...], cl[...])
 
 
 def shards(panel_matrix, trailing):
@@ -470,14 +469,12 @@
         compiler_params=pltpu.CompilerParams(collective_id=0, has_side_effects=True, vmem_limit_bytes=45 * 2**20),
     )(panel_matrix, trailing)
 
-    whole = lambda *s: pl.BlockSpec(s, lambda i: (0,) * len(s))
     rows = lambda *s: pl.BlockSpec(s, lambda i: (i, 0))
-    block = pl.BlockSpec((None, 256, 128), lambda i: (i, 0, 0))
     projected, coupling, r = pl.pallas_call(
         tail_kernel,
         grid=(4,),
         out_shape=(f(1024, 1024), f(512, 1024), f(512, 512)),
-        in_specs=[rows(256, 1024), block, block, whole(512, 1024), whole(512, 512)],
+        in_specs=[V] * 5,
         out_specs=(rows(256, 1024), rows(128, 1024), rows(128, 512)),
         scratch_shapes=[vh(128, 1024), vh(128, 1024)],
         name="project",

time: 73.3 us -> 76 us (1.037)
  Pallas kernels: 71.5 us -> 74.2 us
    pallas_call x1, Pallas kernels: 67.3 us -> 70 us  [shards(): pl.pallas_call(comm_kernel, out_shape=(f(512, 512), f(1024, 1024), h(4, 2...]
where the time goes in v5:
time: 76 us; the launch traced here: 75.9 us
  Pallas kernels  74.2 us (98%)
  local copies, waits for them, and re-layouts  1.03 us (1%)
    pallas_call x1, Pallas kernels, shards(): pl.pallas_call(comm_kernel, out_shape=(f(512, 512), f(1024, 1024), h(4, 2...  70 us
    pallas_call x1, Pallas kernels, shards(): pl.pallas_call(tail_kernel, grid=(4,), out_shape=(f(1024, 1024), f(512, 1...  4.21 us

profile of v5, /device:TPU:1, one launch (start us, length us, event | category | flops | bytes accessed | tf_op | source)
XLA Modules:
  0.0 75.9 jit_solution(17576816289030470506)
XLA Ops:
  0.6 0.0 copy-start
  0.6 1.0 %copy-done = f32[256,512]{1,0:T(8,128)S(1)} copy-done((f32[256,512]{1,0:T(8,128)S(1)}, f32[256,512]{1,0:T(8,128)}, u32[]{:S(2)}) %copy-start) | copy-done | bytes 524312
  1.7 70.0 %reduce_and_factor.1 = (f32[512,512]{1,0:T(8,128)S(1)}, f32[1024,1024]{1,0:T(8,128)S(1)}, bf16[4,256,128]{2,1,0:T(8,128)(2,1)S(1)}, bf16[4,256,128]{2,1,0:T(8,128)(2,1)S(1)}, f32[512,1024]{1,0:T(8,128)S(1)}) custom-call(f32[256,512]{1,0:T(8,128)S(1)} %copy-done, f32[1024,1024]{1,0:T(8,128)} %t_hbm.1), custom_call_target="tpu_custom_call" | custom-call | tf_op jit(solution)/shard_map/reduce_and_factor/pallas_call | solution.py:454
  71.7 4.2 %project.1 = (f32[1024,1024]{1,0:T(8,128)}, f32[512,1024]{1,0:T(8,128)}, f32[512,512]{1,0:T(8,128)}) custom-call(f32[1024,1024]{1,0:T(8,128)S(1)} %get-tuple-element.11.p_ref, bf16[4,256,128]{2,1,0:T(8,128)(2,1)S(1)} %get-tuple-element.12.qh_ref, bf16[4,256,128]{2,1,0:T(8,128)(2,1)S(1)} %get-tuple-element.13.ql_ref, ...), custom_call_target="tpu_custom_call" | custom-call | tf_op jit(solution)/shard_map/project/pallas_call | solution.py:473
Async XLA Ops:
  0.6 1.0 %copy-start = (f32[256,512]{1,0:T(8,128)S(1)}, f32[256,512]{1,0:T(8,128)}, u32[]{:S(2)}) copy-start(f32[256,512]{1,0:T(8,128)} %a_hbm.1) | copy-start | bytes 1572868

commit v6 on v4

--- a/solution.py
+++ b/solution.py
@@ -143,10 +143,11 @@
         k, _, whole = group
         pltpu.make_async_copy(whole, whole, recv.at[k]).wait()
 
-    def sent():
-        for k, _, whole in pending:
+    def sent(but=0):
+        done = pending[: len(pending) - but]
+        for k, _, whole in done:
             pltpu.make_async_copy(whole, whole, send.at[k]).wait()
-        pending.clear()
+        del pending[: len(done)]
 
     def rows_of(n):
         return lambda i: (pl.ds(pl.multiple_of(i * n, 8), n), slice(None))
@@ -361,6 +362,7 @@
             w_third(2)
         if J == 3:
             w_last(1)
+            sent(8)
 
     def at_end(J):
         if J == 0:
@@ -406,28 +408,25 @@
         ah, al = split(ag[rows][:, : cols.stop])
         return split(dot3(ah, al, xth[: cols.stop, cols], xtl[: cols.stop, cols]))
 
-    most, last = slice(0, 384), slice(384, 512)
-    qa = [basis(b, most) for b in range(4)]
+    first, second = slice(0, 256), slice(256, 512)
+    qa = [basis(b, first) for b in range(4)]
     for b in range(4):
-        qh_ref[b], ql_ref[b] = basis(b, last)
+        qh_ref[b], ql_ref[b] = basis(b, second)
     arrive(w5[0])
     arrive(w5[1])
     wh, wl = split(wo[0:2].reshape(256, 1024))
     cpl_a = dot3(xh[:256, :256], xl[:256, :256], wh, wl)
-    cpl_b = dot3(xh[256:, :256], xl[256:, :256], wh, wl)
     cpl_ref[0:256] = cpl_a
     w_last(3)
-    arrive(w5[2])
-    wh, wl = split(wo[2].reshape(128, 1024))
-    cpl_b = cpl_b + dot3(xh[256:, 256:384], xl[256:, 256:384], wh, wl)
-    cpl_ref[256:384] = cpl_b[:128]
-    ch, cl = split(jnp.concatenate([cpl_a, cpl_b[:128]], 0))
+    cpl_b = dot3(xh[256:, :256], xl[256:, :256], wh, wl)
+    ch, cl = split(cpl_a)
     for b in range(4):
         rows = slice(b * 256, b * 256 + 256)
         p_ref[rows] = t_ref[rows] - dot3(*qa[b], ch, cl)
+    arrive(w5[2])
     arrive(w5[3])
-    wh, wl = split(wo[3].reshape(128, 1024))
-    cpl_ref[384:512] = cpl_b[128:] + dot3(xh[384:, 384:], xl[384:, 384:], wh, wl)
+    wh, wl = split(wo[2:4].reshape(256, 1024))
+    cpl_ref[256:512] = cpl_b + dot3(xh[256:, 256:], xl[256:, 256:], wh, wl)
     sent()
 
 
@@ -436,12 +435,13 @@
 
     @pl.when(i == 0)
     def _():
-        ch[...], cl[...] = split(cpl_in[384:512])
+        ch[...], cl[...] = split(cpl_in[256:512])
 
     rows = pl.ds(pl.multiple_of(i * 128, 128), 128)
     cpl_out[...] = cpl_in[rows]
     r_out[...] = r_in[rows]
-    out_ref[...] = p_ref[...] - dot3(qh_ref[...], ql_ref[...], ch[...], cl[...])
+    block = pl.ds(pl.multiple_of(i * 256, 256), 256)
+    out_ref[...] = p_ref[block] - dot3(qh_ref[i], ql_ref[i], ch[...], cl[...])
 
 
 def shards(panel_matrix, trailing):
@@ -454,7 +454,7 @@
     dma = pltpu.SemaphoreType.DMA
     r, part, qh, ql, cpl = pl.pallas_call(
         comm_kernel,
-        out_shape=(f(512, 512), f(1024, 1024), h(4, 256, 128), h(4, 256, 128), f(512, 1024)),
+        out_shape=(f(512, 512), f(1024, 1024), h(4, 256, 256), h(4, 256, 256), f(512, 1024)),
         in_specs=[HBM, HBM],
         out_specs=(V,) * 5,
         scratch_shapes=[
@@ -470,16 +470,14 @@
         compiler_params=pltpu.CompilerParams(collective_id=0, has_side_effects=True, vmem_limit_bytes=45 * 2**20),
     )(panel_matrix, trailing)
 
-    whole = lambda *s: pl.BlockSpec(s, lambda i: (0,) * len(s))
     rows = lambda *s: pl.BlockSpec(s, lambda i: (i, 0))
-    block = pl.BlockSpec((None, 256, 128), lambda i: (i, 0, 0))
     projected, coupling, r = pl.pallas_call(
         tail_kernel,
         grid=(4,),
         out_shape=(f(1024, 1024), f(512, 1024), f(512, 512)),
-        in_specs=[rows(256, 1024), block, block, whole(512, 1024), whole(512, 512)],
+        in_specs=[V] * 5,
         out_specs=(rows(256, 1024), rows(128, 1024), rows(128, 512)),
-        scratch_shapes=[vh(128, 1024), vh(128, 1024)],
+        scratch_shapes=[vh(256, 1024), vh(256, 1024)],
         name="project",
         compiler_params=pltpu.CompilerParams(vmem_limit_bytes=24 * 2**20),
     )(part, qh, ql, cpl, r)

time: 73.3 us -> 73.1 us (level)
  no operation moved by 1% of the time
where the time goes in v6:
time: 73.1 us; the launch traced here: 72.9 us
  Pallas kernels  71.2 us (97%)
  local copies, waits for them, and re-layouts  1.03 us (1%)
    pallas_call x1, Pallas kernels, shards(): pl.pallas_call(comm_kernel, out_shape=(f(512, 512), f(1024, 1024), h(4, 2...  66.9 us
    pallas_call x1, Pallas kernels, shards(): pl.pallas_call(tail_kernel, grid=(4,), out_shape=(f(1024, 1024), f(512, 1...  4.31 us

profile of v6, /device:TPU:1, one launch (start us, length us, event | category | flops | bytes accessed | tf_op | source)
XLA Modules:
  0.0 72.9 jit_solution(15475321023120525644)
XLA Ops:
  0.6 0.0 copy-start
  0.6 1.0 %copy-done = f32[256,512]{1,0:T(8,128)S(1)} copy-done((f32[256,512]{1,0:T(8,128)S(1)}, f32[256,512]{1,0:T(8,128)}, u32[]{:S(2)}) %copy-start) | copy-done | bytes 524312
  1.7 66.9 %reduce_and_factor.1 = (f32[512,512]{1,0:T(8,128)S(1)}, f32[1024,1024]{1,0:T(8,128)S(1)}, bf16[4,256,256]{2,1,0:T(8,128)(2,1)S(1)}, bf16[4,256,256]{2,1,0:T(8,128)(2,1)S(1)}, f32[512,1024]{1,0:T(8,128)S(1)}) custom-call(f32[256,512]{1,0:T(8,128)S(1)} %copy-done, f32[1024,1024]{1,0:T(8,128)} %t_hbm.1), custom_call_target="tpu_custom_call" | custom-call | tf_op jit(solution)/shard_map/reduce_and_factor/pallas_call | solution.py:455
  68.6 4.3 %project.1 = (f32[1024,1024]{1,0:T(8,128)}, f32[512,1024]{1,0:T(8,128)}, f32[512,512]{1,0:T(8,128)}) custom-call(f32[1024,1024]{1,0:T(8,128)S(1)} %get-tuple-element.11.p_ref, bf16[4,256,256]{2,1,0:T(8,128)(2,1)S(1)} %get-tuple-element.12.qh_ref, bf16[4,256,256]{2,1,0:T(8,128)(2,1)S(1)} %get-tuple-element.13.ql_ref, ...), custom_call_target="tpu_custom_call" | custom-call | tf_op jit(solution)/shard_map/project/pallas_call | solution.py:474
Async XLA Ops:
  0.6 1.0 %copy-start = (f32[256,512]{1,0:T(8,128)S(1)}, f32[256,512]{1,0:T(8,128)}, u32[]{:S(2)}) copy-start(f32[256,512]{1,0:T(8,128)} %a_hbm.1) | copy-start | bytes 1572868
